TPU v7x, 256 devices: a whole 4x4x8 slice. The times are simulated.
256 devices in a mesh: az: 128 (over z, y, x), grp: 2 (over core).
Axes of the slice: x: 4, y: 4, z: 8, core: 2. Of those that a mesh axis runs over, the one named last changes fastest.
Arguments:
- features: bfloat16 [256, 512, 128], P(None, 'az', 'grp'), may hold values from -6 to 6
- cotangent: bfloat16 [256, 512, 128], P(None, 'az', 'grp'), may hold values from -6 to 6
- w_first: bfloat16 [256, 6912], P('grp'), may hold values from -0.078125 to 0.078125
- w_second: bfloat16 [256, 6912], P('grp'), may hold values from -0.078125 to 0.078125
Outputs:
- flow_out: bfloat16 [256, 512, 128], P(None, 'az', 'grp')
- grad_first: float32 [256, 6912], P('grp')
- grad_second: float32 [256, 6912], P('grp')
All inputs are finite; a program needn't handle non-finite values.
Results may differ from a plain program's by a relative error of at most 0.01.
Values may be sent and summed in bfloat16 or wider, within the bound.
A program may use at most 128 MiB of HBM per device.

v0:
```python
import math

import jax
import jax.numpy as jnp
from jax import lax
from jax.sharding import PartitionSpec as P

RAD_DEV = 8
AXIAL = 8


def with_halo(cells, sides, width, closed):
    for axis, dim in sides:
        count = lax.axis_size(axis)
        ends = count if closed else count - 1
        head = lax.slice_in_dim(cells, 0, width, axis=dim)
        tail = lax.slice_in_dim(cells, cells.shape[dim] - width, cells.shape[dim], axis=dim)
        cells = jnp.concatenate(
            [
                lax.ppermute(tail, axis, [(i, (i + 1) % count) for i in range(ends)]),
                cells,
                lax.ppermute(head, axis, [((i + 1) % count, i) for i in range(ends)]),
            ],
            axis=dim,
        )
    return cells


def silu_slope(values):
    sigma = jax.nn.sigmoid(values)
    return sigma * (1.0 + values * (1.0 - sigma))


def patches(padded, flipped):
    channels, span_az, span_rad, span_ax = padded.shape
    inner_az = span_az - 2
    inner_rad = span_rad - 2
    inner_ax = span_ax - 2
    stacked = []
    for along_az in range(3):
        for along_rad in range(3):
            for along_ax in range(3):
                if flipped:
                    first_az, first_rad, first_ax = (2 - along_az, 2 - along_rad, 2 - along_ax)
                else:
                    first_az, first_rad, first_ax = (along_az, along_rad, along_ax)
                stacked.append(
                    padded[
                        :,
                        first_az : first_az + inner_az,
                        first_rad : first_rad + inner_rad,
                        first_ax : first_ax + inner_ax,
                    ]
                )
    return jnp.stack(stacked, axis=0).reshape(27 * channels, inner_az * inner_rad * inner_ax)


def az_rim(field):
    return with_halo(field, (("az", 1),), 1, True)


def radial_rim(field):
    return with_halo(field, (("grp", 2),), 1, False)


def axial_pad(field):
    return jnp.pad(field, ((0, 0), (0, 0), (0, 0), (1, 1)))


def flip_weight(weight):
    rows_here = weight.shape[0]
    channels = weight.shape[1] // 27
    return (
        weight.reshape(rows_here, 27, channels).transpose(2, 1, 0).reshape(channels, 27 * rows_here)
    )


def contract_cells(left, right):
    return lax.dot_general(
        left, right, (((1,), (1,)), ((), ())), preferred_element_type=jnp.float32
    )


def rows_forward(weight, columns):
    return jnp.dot(
        lax.all_gather(weight, "grp", axis=0, tiled=True),
        columns,
        preferred_element_type=jnp.float32,
    )


def group_grad(source, columns):
    return lax.psum_scatter(
        contract_cells(source, columns).astype(jnp.bfloat16), "grp", scatter_dimension=0, tiled=True
    ).astype(jnp.float32)


def local(features, cotangent, w_first, w_second):
    channels, az_cells, flat_cells = features.shape
    groups = lax.axis_size("grp")
    cell_count = az_cells * RAD_DEV * AXIAL
    factor = 1.0 / math.sqrt(az_cells * lax.axis_size("az") * RAD_DEV * groups * AXIAL)
    field_in = features.reshape(channels, az_cells, RAD_DEV, AXIAL)
    field_cot = cotangent.reshape(channels, az_cells, RAD_DEV, AXIAL)
    input_columns = patches(axial_pad(radial_rim(az_rim(field_in))), False)
    pre_first = rows_forward(w_first, input_columns).reshape(channels, az_cells, flat_cells)
    hidden = jax.nn.silu(pre_first).astype(jnp.bfloat16)
    hidden_columns = patches(
        axial_pad(radial_rim(az_rim(hidden.reshape(channels, az_cells, RAD_DEV, AXIAL)))), False
    )
    second = rows_forward(w_second, hidden_columns).reshape(channels, az_cells, flat_cells)
    flow_out = (features.astype(jnp.float32) + second).astype(jnp.bfloat16)
    cot_columns = patches(axial_pad(radial_rim(az_rim(field_cot))), True).reshape(
        27, channels, cell_count
    )
    weight_piece = lax.all_gather(w_second, "grp", axis=0, tiled=True)
    piece_rows = weight_piece.shape[0]
    turned = flip_weight(weight_piece)
    picked = cot_columns.reshape(27 * piece_rows, cell_count)
    back_grad = jnp.dot(turned, picked, preferred_element_type=jnp.float32)
    slope = (back_grad * silu_slope(pre_first.reshape(channels, cell_count))).astype(jnp.bfloat16)
    grad_second = group_grad(cotangent.reshape(channels, cell_count), hidden_columns)
    grad_first = group_grad(slope, input_columns)
    grad_first, grad_second = lax.psum((grad_first, grad_second), "az")
    return (flow_out, grad_first * factor, grad_second * factor)


def solution(mesh):
    in_specs = (P(None, "az", "grp"), P(None, "az", "grp"), P("grp", None), P("grp", None))
    out_specs = (P(None, "az", "grp"), P("grp", None), P("grp", None))
    return jax.shard_map(local, mesh=mesh, in_specs=in_specs, out_specs=out_specs, check_vma=False)
```

profile of v0, /device:TPU:8, one launch (start us, length us, event | category | flops | bytes accessed | tf_op | source)
XLA Modules:
  0.0 880.6 jit_solution(9786524235160068136)
XLA Ops:
  7.2 0.0 copy-start.2
  7.2 0.0 copy-start
  7.2 0.0 all-gather.5.cloned.1.call-start
  7.2 3.9 copy.92
  11.1 0.0 all-gather.5.cloned.1.call-update
  11.1 0.0 all-gather.3.cloned.1.call-start
  11.2 0.0 copy-done.2
  11.2 2.7 collective-permute-start.1
  13.9 0.0 collective-permute-start
  13.9 0.0 copy-done
  14.0 4.2 collective-permute-start.9
  18.2 0.0 collective-permute-start.8
  18.2 0.0 all-gather.3.cloned.1.call-update
  18.2 0.0 reduce-scatter.3.cloned.1.call-start
  18.2 0.0 collective-permute-done.1
  18.2 1.7 collective-permute-done
  20.0 1.3 collective-permute-start.3
  21.3 3.0 collective-permute-start.2
  24.3 0.0 collective-permute-done.9
  24.3 0.0 collective-permute-done.8
  24.3 1.3 collective-permute-start.11
  25.6 3.0 collective-permute-start.10
  28.7 0.0 collective-permute-done.3
  28.7 0.0 collective-permute-done.2
  28.7 0.3 fusion.13
  29.8 2.0 copy.97
  31.9 0.0 collective-permute-done.11
  31.9 0.0 collective-permute-done.10
  31.9 0.3 select_maximum_fusion
  33.0 0.2 copy.99
  33.2 0.0 all-gather.5.cloned.1.call-done
  33.3 5.7 copy.94
  39.0 13.9 %all-gather.3.cloned.1.call-done = bf16[256,6912]{1,0:T(8,128)(2,1)} async-done(((bf16[128,6912]{1,0:T(8,128)(2,1)}), bf16[256,6912]{1,0:T(8,128)(2,1)}) %all-gather.3.cloned.1.call-update) | async-done | bytes 3538960 | tf_op jit(solution)/shard_map/all_gather | solution.py:86
  52.9 4.9 fusion.37
  57.7 8.9 %convolution_convert_fusion.1 = bf16[256,6912]{1,0:T(8,128)(2,1)} fusion(bf16[6912,256]{0,1:T(8,128)(2,1)} %bitcast.390, bf16[6912,256]{0,1:T(8,128)(2,1)S(1)} %bitcast.386, bf16[256,6912]{0,1:T(8,128)(2,1)} %bitcast.391, f32[256,256]{1,0:T(8,128)} %fusion.37), kind=kOutput, calls=%fused_computation.1 | convolution fusion | flops 1814298624 | bytes 14417920 | tf_op jit(solution)/shard_map/dot_general | solution.py:79
  66.7 0.0 copy-start.4
  66.7 0.0 reduce-scatter.3.cloned.1.call-update
  66.7 0.0 reduce-scatter.5.cloned.1.call-start
  66.8 0.9 copy-done.4
  67.6 0.1 multiply_convert_fusion.1
  67.7 2.7 collective-permute-start.5
  70.5 0.0 collective-permute-start.4
  70.5 1.6 collective-permute-done.5
  72.1 4.4 collective-permute-done.4
  76.5 1.3 collective-permute-start.7
  77.8 3.0 collective-permute-start.6
  80.8 0.0 collective-permute-done.7
  80.9 0.8 collective-permute-done.6
  81.7 0.3 select_maximum_fusion.4
  82.4 0.1 constant_dynamic-update-slice_fusion.40
  82.9 0.0 copy-start.1
  82.9 0.2 copy.98
  83.1 0.7 copy-done.1
  83.8 2.9 fusion
  86.7 0.0 reduce-scatter.5.cloned.1.call-update
  86.7 0.0 copy-start.3
  86.8 3.1 fusion.38
  89.9 0.0 copy-done.3
  89.9 0.7 add_convert_fusion
  90.6 0.0 reduce-scatter.3.cloned.1.call-done
  90.6 15.4 %reduce-scatter.5.cloned.1.call-done = bf16[128,6912]{1,0:T(8,128)(2,1)} async-done(((bf16[256,6912]{1,0:T(8,128)(2,1)}), bf16[128,6912]{1,0:T(8,128)(2,1)}) %reduce-scatter.5.cloned.1.call-update) | async-done | bytes 1769488 | tf_op jit(solution)/shard_map/reduce_scatter | solution.py:93
  106.0 762.7 %all-reduce.5 = (f32[128,6912]{1,0:T(8,128)S(1)}, f32[128,6912]{1,0:T(8,128)}) all-reduce(bf16[128,6912]{1,0:T(8,128)(2,1)} %reduce-scatter.3.cloned.1.call-done, bf16[128,6912]{1,0:T(8,128)(2,1)} %reduce-scatter.5.cloned.1.call-done), channel_id=1, replica_groups=mesh['az'=128,'grp'=2] {'az'}, use_global_device_ids=true, to_apply=%region_1.2 | all-reduce | flops 1769472 | bytes 10616832 | tf_op jit(solution)/shard_map/psum | solution.py:124
  868.6 5.4 broadcast_multiply_fusion
  (89 shorter events, 1.9 us)
Async XLA Ops:
  7.2 4.0 copy-start.2
  7.2 6.8 copy-start
  7.2 26.1 %all-gather.5.cloned.1.call-start = ((), (), s32[]{:S(2)}) async-start(), calls=%async_computation.3 | async-start | bytes 5308416 | tf_op jit(solution)/shard_map/all_gather | solution.py:86
  11.1 41.7 %all-gather.3.cloned.1.call-start = ((), (), s32[]{:S(2)}) async-start(), calls=%async_computation.2 | async-start | bytes 5308416 | tf_op jit(solution)/shard_map/all_gather | solution.py:86
  11.2 7.0 collective-permute-start.1
  13.9 6.0 collective-permute-start
  14.0 10.4 %collective-permute-start.9 = (bf16[256,1,8,8]{0,3,2,1:T(8,128)(2,1)S(1)}, bf16[256,1,8,8]{0,3,2,1:T(8,128)(2,1)S(1)}, u32[]{:S(2)}, u32[]{:S(2)}) collective-permute-start(bf16[256,1,8,8]{0,3,2,1:T(8,128)(2,1)S(1)} %get-tuple-element.18), channel_id=1, source_target_pairs={{2,0},{4,2},{6,4},{8,6},{10,8},{12,10},{14,12},{16,14},{18,16},{20... | collective-permute-start | bytes 98312 | tf_op jit(solution)/shard_map/ppermute | solution.py:22
  18.2 6.2 collective-permute-start.8
  18.2 72.4 %reduce-scatter.3.cloned.1.call-start = ((), (), s32[]{:S(2)}) async-start(), calls=%async_computation.4 | async-start | bytes 5308416 | tf_op jit(solution)/shard_map/reduce_scatter | solution.py:93
  20.0 8.7 collective-permute-start.3
  21.3 7.4 collective-permute-start.2
  24.3 7.5 collective-permute-start.11
  25.6 6.2 collective-permute-start.10
  66.7 0.9 copy-start.4
  66.7 39.3 %reduce-scatter.5.cloned.1.call-start = ((), (), s32[]{:S(2)}) async-start(), calls=%async_computation.5 | async-start | bytes 5308416 | tf_op jit(solution)/shard_map/reduce_scatter | solution.py:93
  67.7 4.3 collective-permute-start.5
  70.5 6.0 collective-permute-start.4
  76.5 4.3 collective-permute-start.7
  77.8 3.9 collective-permute-start.6
  82.9 0.9 copy-start.1
  86.7 3.1 copy-start.3
Sparse Core Ops, SparseCore 0:
  11.3 20.4 all-gather.4
  33.5 19.2 all-gather.2
  66.8 18.0 reduce-scatter.2
  88.0 17.9 reduce-scatter.4
where the time goes:
time: 890 us; the launch traced here: 881 us
  blocking collectives  763 us (86%)
  waiting for transfers between devices  37.9 us (4%)
  starting transfers between devices  22.8 us (3%)
  matrix products  19.9 us (2%)
  local copies, waits for them, and re-layouts  15.4 us (2%)
  between operations  14.6 us (2%)
    psum x1, blocking collectives, local(): grad_first, grad_second = lax.psum((grad_first, grad_second), 'az')  763 us
  transfers between devices with their start and end apart: 16, of which 6 were waited for; matrix products, arithmetic and copies ran while one was open for 2% of the time, Pallas kernels for 0%

commit v1 on v0

--- a/solution.py
+++ b/solution.py
@@ -1,8 +1,11 @@
+import functools
 import math
 
 import jax
 import jax.numpy as jnp
 from jax import lax
+from jax.experimental import pallas as pl
+from jax.experimental.pallas import tpu as pltpu
 from jax.sharding import PartitionSpec as P
 
 RAD_DEV = 8
@@ -92,7 +95,223 @@
 def group_grad(source, columns):
     return lax.psum_scatter(
         contract_cells(source, columns).astype(jnp.bfloat16), "grp", scatter_dimension=0, tiled=True
-    ).astype(jnp.float32)
+    )
+
+
+NX, NY, NZ = 4, 4, 8
+EXTENT = {"x": NX, "y": NY, "z": NZ}
+TAP_LANES = 128
+PARTS = (
+    ("z", "y", "x", 0, 4, True),
+    ("z", "y", "x", 4, 3, False),
+    ("x", "z", "y", 7, 5, True),
+    ("x", "z", "y", 12, 5, False),
+    ("y", "z", "x", 17, 5, True),
+    ("y", "z", "x", 22, 5, False),
+)
+
+
+def chain_lengths(axis, longer_below):
+    count = EXTENT[axis]
+    longer, shorter = count // 2, count - 1 - count // 2
+    return (longer, shorter) if longer_below else (shorter, longer)
+
+
+def chunk_shape(axes_done, axis, taps):
+    rows = 16 if "z" in axes_done + (axis,) else 128
+    lead = () if ("x" in axes_done + (axis,) or "y" in axes_done + (axis,)) else (4,)
+    return lead + (rows, taps * TAP_LANES)
+
+
+class Links:
+    def __init__(self, send_sems, recv_sems):
+        self.send_sems, self.recv_sems, self.used, self.started = send_sems, recv_sems, 0, []
+        flat = lax.axis_index("az")
+        self.at = {"x": flat % NX, "y": (flat // NX) % NY, "z": flat // (NX * NY)}
+
+    def index(self, axis, shift):
+        return (self.at[axis] + (shift + EXTENT[axis])) % EXTENT[axis]
+
+    def peer(self, axis, shift):
+        to = dict(self.at)
+        to[axis] = self.index(axis, shift)
+        return {"az": (to["z"] * NY + to["y"]) * NX + to["x"]}
+
+    def copy(self, source, target, axis, shift):
+        number = self.used
+        self.used += 1
+        handle = pltpu.make_async_remote_copy(
+            src_ref=source,
+            dst_ref=target,
+            send_sem=self.send_sems.at[number],
+            recv_sem=self.recv_sems.at[number],
+            device_id=self.peer(axis, shift),
+            device_id_type=pl.DeviceIdType.MESH,
+        )
+        handle.start()
+        self.started.append(handle)
+        return handle
+
+
+def piece(ref, axes, at, lanes):
+    rows = pl.ds(0, 128)
+    if "z" in axes:
+        rows = pl.ds(pl.multiple_of(at["z"] * 16, 16), 16)
+    lead = [a for a in axes if a != "z"]
+    first = at[lead[0]] if lead else slice(None)
+    return ref.at[first, rows, lanes]
+
+
+def scatter_axis(links, axis, longer_below, own, buffers):
+    below, above = chain_lengths(axis, longer_below)
+    ways = [(1, below, buffers[0], buffers[1]), (-1, above, buffers[2], buffers[3])]
+    last = {}
+    for step in range(1, max(below, above) + 1):
+        for sense, length, stage, landing in ways:
+            if step > length:
+                continue
+            total = own(links.index(axis, sense * (length - step + 1)))
+            if step > 1:
+                last[sense].wait_recv()
+                total = total + landing[step - 2].astype(jnp.float32)
+            stage[step - 1] = total.astype(jnp.bfloat16)
+            last[sense] = links.copy(stage.at[step - 1], landing.at[step - 1], axis, sense)
+        yield
+    total = own(links.at[axis])
+    for sense, length, stage, landing in ways:
+        last[sense].wait_recv()
+        total = total + landing[length - 1].astype(jnp.float32)
+    return total
+
+
+def gather_axis(links, axis, longer_below, view):
+    below, above = chain_lengths(axis, longer_below)
+    last = {}
+    for step in range(1, max(below, above) + 1):
+        for sense, length in ((1, below), (-1, above)):
+            if step > length:
+                continue
+            if step > 1:
+                last[sense].wait_recv()
+            chunk = view(links.index(axis, -sense * (step - 1)))
+            last[sense] = links.copy(chunk, chunk, axis, sense)
+        yield
+    for sense in (1, -1):
+        last[sense].wait_recv()
+
+
+def reduce_part(links, part, source, result, buffers):
+    first, second, third, tap, taps, longer_below = part
+    lanes = pl.ds(tap * TAP_LANES, taps * TAP_LANES)
+    one, two, three = buffers[:5], buffers[5:10], buffers[10:]
+
+    def own_first(index):
+        return piece(source, (first,), {first: index}, lanes)[...].astype(jnp.float32)
+
+    total = yield from scatter_axis(links, first, longer_below, own_first, one[:4])
+    one[4][...] = total
+
+    def own_second(index):
+        if second == "z":
+            return one[4][pl.ds(pl.multiple_of(index * 16, 16), 16), :]
+        return one[4][index]
+
+    total = yield from scatter_axis(links, second, not longer_below, own_second, two[:4])
+    mine, landing = three
+    landing[links.at[third]] = total.astype(jnp.bfloat16)
+    handles = [
+        links.copy(landing.at[links.at[third]], landing.at[links.at[third]], third, shift)
+        for shift in (1, -1, 2)
+    ]
+    yield
+    for handle in handles:
+        handle.wait_recv()
+    total = landing[0].astype(jnp.float32)
+    for index in range(1, EXTENT[third]):
+        total = total + landing[index].astype(jnp.float32)
+    piece(result, (first, second), links.at, lanes)[...] = total.astype(jnp.bfloat16)
+    at = links.at
+    yield from gather_axis(
+        links,
+        second,
+        longer_below,
+        lambda index: piece(result, (first, second), {**at, second: index}, lanes),
+    )
+    yield from gather_axis(
+        links,
+        first,
+        not longer_below,
+        lambda index: piece(result, (first,), {**at, first: index}, lanes),
+    )
+
+
+def part_scratch(part):
+    first, second, third, tap, taps, longer_below = part
+    shapes = []
+    one = chunk_shape((), first, taps)
+    two = chunk_shape((first,), second, taps)
+    for axis, shape, flag in ((first, one, longer_below), (second, two, not longer_below)):
+        below, above = chain_lengths(axis, flag)
+        for length in (below, below, above, above):
+            shapes.append(pltpu.VMEM((length,) + shape, jnp.bfloat16))
+        shapes.append(pltpu.VMEM(shape, jnp.float32))
+    shapes.append(pltpu.VMEM((8, 128), jnp.float32))
+    shapes.append(pltpu.VMEM((EXTENT[third],) + two, jnp.bfloat16))
+    return shapes
+
+
+def greet(links):
+    barrier = pltpu.get_barrier_semaphore()
+    peers = [("z", 1), ("z", -1)] + [(axis, shift) for axis in "xy" for shift in (1, -1, 2)]
+    for axis, shift in peers:
+        pl.semaphore_signal(
+            barrier,
+            inc=1,
+            device_id=links.peer(axis, shift),
+            device_id_type=pl.DeviceIdType.MESH,
+        )
+    pl.semaphore_wait(barrier, len(peers))
+
+
+COPIES = 256
+
+
+def reduce_kernel(source, result, send_sems, recv_sems, *buffers):
+    links = Links(send_sems, recv_sems)
+    greet(links)
+    running, used = [], 0
+    for part in PARTS:
+        count = len(part_scratch(part))
+        running.append(reduce_part(links, part, source, result, buffers[used : used + count]))
+        used += count
+    while running:
+        left = []
+        for one in running:
+            try:
+                next(one)
+                left.append(one)
+            except StopIteration:
+                pass
+        running = left
+    for handle in links.started:
+        handle.wait_send()
+
+
+def reduce_over_az(terms):
+    scratch = [pltpu.SemaphoreType.DMA((COPIES,)), pltpu.SemaphoreType.DMA((COPIES,))]
+    for part in PARTS:
+        scratch += part_scratch(part)
+    return pl.pallas_call(
+        reduce_kernel,
+        out_shape=jax.ShapeDtypeStruct(terms.shape, jnp.bfloat16),
+        in_specs=[pl.BlockSpec(memory_space=pltpu.VMEM)],
+        out_specs=pl.BlockSpec(memory_space=pltpu.VMEM),
+        scratch_shapes=scratch,
+        compiler_params=pltpu.CompilerParams(
+            collective_id=0, has_side_effects=True, vmem_limit_bytes=40 * 2**20
+        ),
+        name="reduce_over_az",
+    )(terms)
 
 
 def local(features, cotangent, w_first, w_second):
@@ -121,8 +340,12 @@
     slope = (back_grad * silu_slope(pre_first.reshape(channels, cell_count))).astype(jnp.bfloat16)
     grad_second = group_grad(cotangent.reshape(channels, cell_count), hidden_columns)
     grad_first = group_grad(slope, input_columns)
-    grad_first, grad_second = lax.psum((grad_first, grad_second), "az")
-    return (flow_out, grad_first * factor, grad_second * factor)
+    rows = grad_first.shape[0]
+    terms = jnp.stack((grad_first, grad_second)).reshape(2, rows, 27, 2, 128)
+    summed = reduce_over_az(terms.transpose(0, 3, 1, 2, 4).reshape(4, rows, 27 * 128))
+    summed = summed.reshape(2, 2, rows, 27, 128).transpose(0, 2, 3, 1, 4).reshape(2, rows, 6912)
+    summed = summed.astype(jnp.float32) * factor
+    return (flow_out, summed[0], summed[1])
 
 
 def solution(mesh):

time: 890 us -> 225 us (0.25)
  blocking collectives: 763 us -> 0 us
  Pallas kernels: 0 us -> 66.7 us
  local copies, waits for them, and re-layouts: 15.4 us -> 59.3 us
    psum x1 -> x0, blocking collectives: 763 us -> none  [local(): grad_first, grad_second = lax.psum((grad_first, grad_second), 'az')]
    pallas_call x0 -> x1, Pallas kernels: none -> 66.7 us  [reduce_over_az(): pl.pallas_call(reduce_kernel, out_shape=jax.ShapeDtypeStruct(terms.shape,...]
    unnamed x85 -> x89, local copies, waits for them, and re-layouts: 9.52 us -> 28.5 us
    reduce_scatter x2 -> x1, waiting for transfers between devices: 15.4 us -> 0.01 us  [group_grad(): lax.psum_scatter(contract_cells(source, columns).astype(jnp.bfloat16), 'g...]
    unnamed x4 -> x5, waiting for transfers between devices: 0.07 us -> 12.2 us
  transfers between devices with their start and end apart: 16 -> 16, of which waited for: 6 -> 6; matrix products, arithmetic and copies ran while one was open for 2% -> 12% of each run, Pallas kernels for 0% -> 0%
where the time goes in v1:
time: 225 us; the launch traced here: 224 us
  Pallas kernels  66.7 us (30%)
  local copies, waits for them, and re-layouts  59.3 us (26%)
  waiting for transfers between devices  34.7 us (15%)
  starting transfers between devices  22.8 us (10%)
  matrix products  19.9 us (9%)
  between operations  14.7 us (7%)
  other arithmetic  5.6 us (2%)
    pallas_call x1, Pallas kernels, reduce_over_az(): pl.pallas_call(reduce_kernel, out_shape=jax.ShapeDtypeStruct(terms.shape,...  66.7 us
    unnamed x89, local copies, waits for them, and re-layouts  28.5 us
    all_gather x2, waiting for transfers between devices, rows_forward(): lax.all_gather(weight, 'grp', axis=0, tiled=True)  13.9 us
    ppermute x6, starting transfers between devices, with_halo(): lax.ppermute(head, axis, [((i + 1) % count, i) for i in range(ends)])  13.6 us
    unnamed x5, waiting for transfers between devices  12.2 us
    dot_general x2, matrix products, contract_cells(): lax.dot_general(left, right, (((1,), (1,)), ((), ())), preferred_element_...  11.9 us
    ppermute x6, starting transfers between devices, with_halo(): lax.ppermute(tail, axis, [(i, (i + 1) % count) for i in range(ends)])  9.09 us
    dot_general x2, matrix products, rows_forward(): jnp.dot(lax.all_gather(weight, 'grp', axis=0, tiled=True), columns, prefe...  8.03 us
  transfers between devices with their start and end apart: 16, of which 6 were waited for; matrix products, arithmetic and copies ran while one was open for 12% of the time, Pallas kernels for 0%

profile of v1, /device:TPU:8, one launch (start us, length us, event | category | flops | bytes accessed | tf_op | source)
XLA Modules:
  0.0 223.6 jit_solution(3494734300775050391)
XLA Ops:
  7.2 0.0 copy-start.2
  7.2 0.0 copy-start
  7.2 0.0 all-gather.5.cloned.1.call-start
  7.2 3.9 %copy.123 = bf16[128,6912]{0,1:T(8,128)(2,1)} copy(bf16[128,6912]{1,0:T(8,128)(2,1)} %param.7) | data formatting | bytes 3538944 | tf_op args[3]
  11.1 0.0 all-gather.5.cloned.1.call-update
  11.1 0.0 all-gather.3.cloned.1.call-start
  11.2 2.7 %collective-permute-start.1 = (bf16[256,1,8,8]{0,3,2,1:T(8,128)(2,1)S(1)}, bf16[256,1,8,8]{0,3,2,1:T(8,128)(2,1)S(1)}, u32[]{:S(2)}, u32[]{:S(2)}) collective-permute-start(bf16[256,1,8,8]{0,3,2,1:T(8,128)(2,1)S(1)} %get-tuple-element.31), channel_id=1, source_target_pairs={{2,0},{4,2},{6,4},{8,6},{10,8},{12,10},{14,12},{16,14},{18,16},{20... | collective-permute-start | bytes 98312 | tf_op jit(solution)/shard_map/ppermute | solution.py:25
  13.9 0.0 collective-permute-start
  14.0 4.2 %collective-permute-start.9 = (bf16[256,1,8,8]{0,3,2,1:T(8,128)(2,1)S(1)}, bf16[256,1,8,8]{0,3,2,1:T(8,128)(2,1)S(1)}, u32[]{:S(2)}, u32[]{:S(2)}) collective-permute-start(bf16[256,1,8,8]{0,3,2,1:T(8,128)(2,1)S(1)} %get-tuple-element.27), channel_id=1, source_target_pairs={{2,0},{4,2},{6,4},{8,6},{10,8},{12,10},{14,12},{16,14},{18,16},{20... | collective-permute-start | bytes 98312 | tf_op jit(solution)/shard_map/ppermute | solution.py:25
  18.2 0.0 all-gather.3.cloned.1.call-update
  18.2 0.0 reduce-scatter.5.cloned.1.call-start
  18.2 1.7 collective-permute-done
  20.0 1.3 collective-permute-start.3
  21.3 3.0 %collective-permute-start.2 = (bf16[256,6,1,8]{0,3,2,1:T(8,128)(2,1)S(1)}, bf16[256,6,1,8]{0,3,2,1:T(8,128)(2,1)S(1)}, u32[]{:S(2)}, u32[]{:S(2)}) collective-permute-start(bf16[256,6,1,8]{0,3,2,1:T(8,128)(2,1)S(1)} %get-tuple-element.24), channel_id=1, source_target_pairs={{0,1},{2,3},{4,5},{6,7},{8,9},{10,11},{12,13},{14,15},{16,17},{18,... | collective-permute-start | bytes 73736 | tf_op jit(solution)/shard_map/ppermute | solution.py:23
  24.3 0.0 collective-permute-done.8
  24.3 1.3 collective-permute-start.11
  25.6 3.0 %collective-permute-start.10 = (bf16[256,6,1,8]{0,3,2,1:T(8,128)(2,1)S(1)}, bf16[256,6,1,8]{0,3,2,1:T(8,128)(2,1)S(1)}, u32[]{:S(2)}, u32[]{:S(2)}) collective-permute-start(bf16[256,6,1,8]{0,3,2,1:T(8,128)(2,1)S(1)} %get-tuple-element.16), channel_id=1, source_target_pairs={{0,1},{2,3},{4,5},{6,7},{8,9},{10,11},{12,13},{14,15},{16,17},{18,... | collective-permute-start | bytes 73736 | tf_op jit(solution)/shard_map/ppermute | solution.py:23
  28.7 0.0 collective-permute-done.3
  28.7 0.0 collective-permute-done.2
  28.7 0.3 fusion.13
  29.8 2.0 copy.137
  31.9 0.3 select_maximum_fusion
  33.0 0.2 copy.139
  33.2 0.0 all-gather.5.cloned.1.call-done
  33.3 5.7 %copy.125 = bf16[256,27,256]{0,2,1:T(8,128)(2,1)} copy(bf16[256,27,256]{2,0,1:T(8,128)(2,1)} %bitcast.425) | data formatting | bytes 7077888 | tf_op jit(solution)/shard_map/transpose | solution.py:77
  39.0 13.9 %all-gather.3.cloned.1.call-done = bf16[256,6912]{1,0:T(8,128)(2,1)} async-done(((bf16[128,6912]{1,0:T(8,128)(2,1)}), bf16[256,6912]{1,0:T(8,128)(2,1)}) %all-gather.3.cloned.1.call-update) | async-done | bytes 3538960 | tf_op jit(solution)/shard_map/all_gather | solution.py:89
  52.9 4.9 %fusion.38 = f32[256,256]{1,0:T(8,128)} fusion(bf16[6912,256]{0,1:T(8,128)(2,1)} %bitcast.404, bf16[256,6912]{1,0:T(8,128)(2,1)} %all-gather.3.cloned.1.call-done), kind=kOutput, calls=%fused_computation.228 | convolution fusion | flops 905969664 | bytes 7340032 | tf_op jit(solution)/shard_map/dot_general | solution.py:88
  57.8 8.9 %convolution_convert_fusion.1 = bf16[256,6912]{1,0:T(8,128)(2,1)} fusion(bf16[6912,256]{0,1:T(8,128)(2,1)} %bitcast.405, bf16[6912,256]{0,1:T(8,128)(2,1)S(1)} %bitcast.397, bf16[256,6912]{0,1:T(8,128)(2,1)} %bitcast.406, f32[256,256]{1,0:T(8,128)} %fusion.38), kind=kOutput, calls=%fused_computation.1 | convolution fusion | flops 1814298624 | bytes 14417920 | tf_op jit(solution)/shard_map/dot_general | solution.py:82
  66.7 0.0 reduce-scatter.5.cloned.1.call-update
  66.7 0.0 reduce-scatter.7.cloned.1.call-start
  66.8 0.9 copy-done.4
  67.7 0.1 multiply_convert_fusion.1
  67.8 2.7 %collective-permute-start.5 = (bf16[256,1,8,8]{0,3,2,1:T(8,128)(2,1)S(1)}, bf16[256,1,8,8]{0,3,2,1:T(8,128)(2,1)S(1)}, u32[]{:S(2)}, u32[]{:S(2)}) collective-permute-start(bf16[256,1,8,8]{0,3,2,1:T(8,128)(2,1)S(1)} %get-tuple-element.29), channel_id=1, source_target_pairs={{2,0},{4,2},{6,4},{8,6},{10,8},{12,10},{14,12},{16,14},{18,16},{20... | collective-permute-start | bytes 98312 | tf_op jit(solution)/shard_map/ppermute | solution.py:25
  70.5 0.0 collective-permute-start.4
  70.5 1.6 collective-permute-done.5
  72.1 4.4 %collective-permute-done.4 = bf16[256,1,8,8]{0,3,2,1:T(8,128)(2,1)S(1)} collective-permute-done((bf16[256,1,8,8]{0,3,2,1:T(8,128)(2,1)S(1)}, bf16[256,1,8,8]{0,3,2,1:T(8,128)(2,1)S(1)}, u32[]{:S(2)}, u32[]{:S(2)}) %collective-permute-start.4) | collective-permute-done | bytes 32800 | tf_op jit(solution)/shard_map/ppermute | solution.py:23
  76.5 1.3 collective-permute-start.7
  77.8 3.0 %collective-permute-start.6 = (bf16[256,6,1,8]{0,3,2,1:T(8,128)(2,1)S(1)}, bf16[256,6,1,8]{0,3,2,1:T(8,128)(2,1)S(1)}, u32[]{:S(2)}, u32[]{:S(2)}) collective-permute-start(bf16[256,6,1,8]{0,3,2,1:T(8,128)(2,1)S(1)} %get-tuple-element.20), channel_id=1, source_target_pairs={{0,1},{2,3},{4,5},{6,7},{8,9},{10,11},{12,13},{14,15},{16,17},{18,... | collective-permute-start | bytes 73736 | tf_op jit(solution)/shard_map/ppermute | solution.py:23
  80.9 0.8 collective-permute-done.6
  81.8 0.3 select_maximum_fusion.4
  82.4 0.1 constant_dynamic-update-slice_fusion.40
  82.9 0.0 copy-start.1
  82.9 0.2 copy.138
  83.1 0.7 copy-done.1
  83.8 2.9 %fusion = bf16[256,6912]{0,1:T(8,128)(2,1)} fusion(bf16[6912,256]{0,1:T(8,128)(2,1)S(1)} %bitcast.399, bf16[256,256]{0,1:T(8,128)(2,1)S(1)} %bitcast.413), kind=kOutput, calls=%fused_computation.2 | convolution fusion | flops 907739136 | bytes 7208960 | tf_op jit(solution)/shard_map/dot_general | solution.py:82
  86.8 6.0 %copy.135 = bf16[256,6912]{1,0:T(8,128)(2,1)} copy(bf16[256,6912]{0,1:T(8,128)(2,1)} %fusion) | data formatting | bytes 7077888
  92.7 0.0 reduce-scatter.7.cloned.1.call-update
  92.7 0.0 copy-start.3
  92.7 3.1 %fusion.39 = f32[256,256]{1,0:T(8,128)S(1)} fusion(bf16[6912,256]{0,1:T(8,128)(2,1)S(1)} %bitcast.400, bf16[256,6912]{0,1:T(8,128)(2,1)} %all-gather.5.cloned.1.call-done), kind=kOutput, calls=%fused_computation.229 | convolution fusion | flops 905969664 | bytes 7340032 | tf_op jit(solution)/shard_map/dot_general | solution.py:88
  95.9 0.7 add_convert_fusion
  96.6 2.7 %copy.134 = bf16[128,6912]{0,1:T(8,128)(2,1)S(1)} copy(bf16[128,6912]{1,0:T(8,128)(2,1)} %reduce-scatter.5.cloned.1.call-done) | data formatting | bytes 3538944 | tf_op jit(solution)/shard_map/stack | solution.py:344
  99.3 12.1 %reduce-scatter.7.cloned.1.call-done = bf16[128,6912]{1,0:T(8,128)(2,1)} async-done(((bf16[256,6912]{1,0:T(8,128)(2,1)}), bf16[128,6912]{1,0:T(8,128)(2,1)}) %reduce-scatter.7.cloned.1.call-update) | async-done | bytes 1769488
  111.4 2.7 %copy.136 = bf16[128,6912]{0,1:T(8,128)(2,1)S(1)} copy(bf16[128,6912]{1,0:T(8,128)(2,1)} %reduce-scatter.7.cloned.1.call-done) | data formatting | bytes 3538944
  114.2 0.3 maximum_bitcast_fusion
  114.5 2.2 copy.127
  116.8 4.3 %copy.128.source = bf16[4,128,3456]{2,1,0:T(8,128)(2,1)S(1)} copy(bf16[4,128,3456]{1,2,0:T(8,128)(2,1)} %bitcast.401) | data formatting | bytes 7077888 | tf_op jit(solution)/shard_map/reshape | solution.py:345
  121.1 66.7 %reduce_over_az.1 = bf16[4,128,3456]{2,1,0:T(8,128)(2,1)S(1)} custom-call(bf16[4,128,3456]{2,1,0:T(8,128)(2,1)S(1)} %copy.128.source), custom_call_target="tpu_custom_call" | custom-call | tf_op jit(solution)/shard_map/reduce_over_az/pallas_call | solution.py:304
  187.8 3.4 %convert_multiply_fusion = f32[4,128,3456]{2,1,0:T(8,128)} fusion(bf16[4,128,3456]{2,1,0:T(8,128)(2,1)S(1)} %reduce_over_az.1), kind=kLoop, calls=%fused_computation.3 | loop fusion | flops 3538944 | bytes 10616832 | tf_op jit(solution)/shard_map/mul | solution.py:347
  191.2 8.0 %copy.129 = f32[4,128,3456]{1,2,0:T(8,128)} copy(f32[4,128,3456]{2,1,0:T(8,128)} %convert_multiply_fusion) | data formatting | bytes 14155776 | tf_op jit(solution)/shard_map/mul | solution.py:347
  199.2 3.6 %fusion.34 = (f32[1,128,27,2,128]{1,4,2,3,0:T(8,128)S(1)}, f32[1,128,27,2,128]{1,4,2,3,0:T(8,128)S(1)}) fusion(f32[2,128,27,2,128]{1,4,2,3,0:T(8,128)} %bitcast.398), kind=kLoop, calls=%fused_computation.224 | loop fusion | bytes 14155776 | tf_op jit(solution)/shard_map/slice | solution.py:348
  202.8 2.0 copy.130
  204.8 5.2 %copy.132 = f32[128,6912]{1,0:T(8,128)} copy(f32[128,6912]{0,1:T(8,128)} %bitcast.402) | data formatting | bytes 7077888
  210.0 2.0 copy.131
  212.0 5.2 %copy.133 = f32[128,6912]{1,0:T(8,128)} copy(f32[128,6912]{0,1:T(8,128)} %bitcast.403) | data formatting | bytes 7077888
  (100 shorter events, 2.0 us)
Async XLA Ops:
  7.2 4.0 %copy-start.2 = (bf16[256,4,64]{0,2,1:T(8,128)(2,1)S(1)}, bf16[256,4,64]{0,2,1:T(8,128)(2,1)}, u32[]{:S(2)}) copy-start(bf16[256,4,64]{0,2,1:T(8,128)(2,1)} %param.4) | copy-start | bytes 393220
  7.2 6.8 %copy-start = (bf16[256,4,64]{0,2,1:T(8,128)(2,1)S(1)}, bf16[256,4,64]{0,2,1:T(8,128)(2,1)}, u32[]{:S(2)}) copy-start(bf16[256,4,64]{0,2,1:T(8,128)(2,1)} %param.5) | copy-start | bytes 393220
  7.2 26.1 %all-gather.5.cloned.1.call-start = ((), (), s32[]{:S(2)}) async-start(), calls=%async_computation.3 | async-start | bytes 5308416 | tf_op jit(solution)/shard_map/all_gather | solution.py:89
  11.1 41.7 %all-gather.3.cloned.1.call-start = ((), (), s32[]{:S(2)}) async-start(), calls=%async_computation.2 | async-start | bytes 5308416 | tf_op jit(solution)/shard_map/all_gather | solution.py:89
  11.2 7.0 %collective-permute-start.1 = (bf16[256,1,8,8]{0,3,2,1:T(8,128)(2,1)S(1)}, bf16[256,1,8,8]{0,3,2,1:T(8,128)(2,1)S(1)}, u32[]{:S(2)}, u32[]{:S(2)}) collective-permute-start(bf16[256,1,8,8]{0,3,2,1:T(8,128)(2,1)S(1)} %get-tuple-element.31), channel_id=1, source_target_pairs={{2,0},{4,2},{6,4},{8,6},{10,8},{12,10},{14,12},{16,14},{18,16},{20... | collective-permute-start | bytes 98312 | tf_op jit(solution)/shard_map/ppermute | solution.py:25
  13.9 6.0 %collective-permute-start = (bf16[256,1,8,8]{0,3,2,1:T(8,128)(2,1)S(1)}, bf16[256,1,8,8]{0,3,2,1:T(8,128)(2,1)S(1)}, u32[]{:S(2)}, u32[]{:S(2)}) collective-permute-start(bf16[256,1,8,8]{0,3,2,1:T(8,128)(2,1)S(1)} %get-tuple-element.30), channel_id=1, source_target_pairs={{0,2},{2,4},{4,6},{6,8},{8,10},{10,12},{12,14},{14,16},{16,18},{18... | collective-permute-start | bytes 98312 | tf_op jit(solution)/shard_map/ppermute | solution.py:23
  14.0 10.4 %collective-permute-start.9 = (bf16[256,1,8,8]{0,3,2,1:T(8,128)(2,1)S(1)}, bf16[256,1,8,8]{0,3,2,1:T(8,128)(2,1)S(1)}, u32[]{:S(2)}, u32[]{:S(2)}) collective-permute-start(bf16[256,1,8,8]{0,3,2,1:T(8,128)(2,1)S(1)} %get-tuple-element.27), channel_id=1, source_target_pairs={{2,0},{4,2},{6,4},{8,6},{10,8},{12,10},{14,12},{16,14},{18,16},{20... | collective-permute-start | bytes 98312 | tf_op jit(solution)/shard_map/ppermute | solution.py:25
  18.2 6.2 %collective-permute-start.8 = (bf16[256,1,8,8]{0,3,2,1:T(8,128)(2,1)S(1)}, bf16[256,1,8,8]{0,3,2,1:T(8,128)(2,1)S(1)}, u32[]{:S(2)}, u32[]{:S(2)}) collective-permute-start(bf16[256,1,8,8]{0,3,2,1:T(8,128)(2,1)S(1)} %get-tuple-element.26), channel_id=1, source_target_pairs={{0,2},{2,4},{4,6},{6,8},{8,10},{10,12},{12,14},{14,16},{16,18},{18... | collective-permute-start | bytes 98312 | tf_op jit(solution)/shard_map/ppermute | solution.py:23
  18.2 78.4 %reduce-scatter.5.cloned.1.call-start = ((), (), s32[]{:S(2)}) async-start(), calls=%async_computation.4 | async-start | bytes 5308416 | tf_op jit(solution)/shard_map/reduce_scatter | solution.py:96
  20.0 8.7 %collective-permute-start.3 = (bf16[256,6,1,8]{0,3,2,1:T(8,128)(2,1)S(1)}, bf16[256,6,1,8]{0,3,2,1:T(8,128)(2,1)S(1)}, u32[]{:S(2)}, u32[]{:S(2)}) collective-permute-start(bf16[256,6,1,8]{0,3,2,1:T(8,128)(2,1)S(1)} %get-tuple-element.25), channel_id=1, source_target_pairs={{1,0},{3,2},{5,4},{7,6},{9,8},{11,10},{13,12},{15,14},{17,16},{19,... | collective-permute-start | bytes 73736 | tf_op jit(solution)/shard_map/ppermute | solution.py:25
  21.3 7.4 %collective-permute-start.2 = (bf16[256,6,1,8]{0,3,2,1:T(8,128)(2,1)S(1)}, bf16[256,6,1,8]{0,3,2,1:T(8,128)(2,1)S(1)}, u32[]{:S(2)}, u32[]{:S(2)}) collective-permute-start(bf16[256,6,1,8]{0,3,2,1:T(8,128)(2,1)S(1)} %get-tuple-element.24), channel_id=1, source_target_pairs={{0,1},{2,3},{4,5},{6,7},{8,9},{10,11},{12,13},{14,15},{16,17},{18,... | collective-permute-start | bytes 73736 | tf_op jit(solution)/shard_map/ppermute | solution.py:23
  24.3 7.5 %collective-permute-start.11 = (bf16[256,6,1,8]{0,3,2,1:T(8,128)(2,1)S(1)}, bf16[256,6,1,8]{0,3,2,1:T(8,128)(2,1)S(1)}, u32[]{:S(2)}, u32[]{:S(2)}) collective-permute-start(bf16[256,6,1,8]{0,3,2,1:T(8,128)(2,1)S(1)} %get-tuple-element.17), channel_id=1, source_target_pairs={{1,0},{3,2},{5,4},{7,6},{9,8},{11,10},{13,12},{15,14},{17,16},{19,... | collective-permute-start | bytes 73736 | tf_op jit(solution)/shard_map/ppermute | solution.py:25
  25.6 6.2 %collective-permute-start.10 = (bf16[256,6,1,8]{0,3,2,1:T(8,128)(2,1)S(1)}, bf16[256,6,1,8]{0,3,2,1:T(8,128)(2,1)S(1)}, u32[]{:S(2)}, u32[]{:S(2)}) collective-permute-start(bf16[256,6,1,8]{0,3,2,1:T(8,128)(2,1)S(1)} %get-tuple-element.16), channel_id=1, source_target_pairs={{0,1},{2,3},{4,5},{6,7},{8,9},{10,11},{12,13},{14,15},{16,17},{18,... | collective-permute-start | bytes 73736 | tf_op jit(solution)/shard_map/ppermute | solution.py:23
  66.7 0.9 copy-start.4
  66.7 44.7 %reduce-scatter.7.cloned.1.call-start = ((), (), s32[]{:S(2)}) async-start(), calls=%async_computation.5 | async-start | bytes 5308416
  67.8 4.3 %collective-permute-start.5 = (bf16[256,1,8,8]{0,3,2,1:T(8,128)(2,1)S(1)}, bf16[256,1,8,8]{0,3,2,1:T(8,128)(2,1)S(1)}, u32[]{:S(2)}, u32[]{:S(2)}) collective-permute-start(bf16[256,1,8,8]{0,3,2,1:T(8,128)(2,1)S(1)} %get-tuple-element.29), channel_id=1, source_target_pairs={{2,0},{4,2},{6,4},{8,6},{10,8},{12,10},{14,12},{16,14},{18,16},{20... | collective-permute-start | bytes 98312 | tf_op jit(solution)/shard_map/ppermute | solution.py:25
  70.5 6.0 %collective-permute-start.4 = (bf16[256,1,8,8]{0,3,2,1:T(8,128)(2,1)S(1)}, bf16[256,1,8,8]{0,3,2,1:T(8,128)(2,1)S(1)}, u32[]{:S(2)}, u32[]{:S(2)}) collective-permute-start(bf16[256,1,8,8]{0,3,2,1:T(8,128)(2,1)S(1)} %get-tuple-element.28), channel_id=1, source_target_pairs={{0,2},{2,4},{4,6},{6,8},{8,10},{10,12},{12,14},{14,16},{16,18},{18... | collective-permute-start | bytes 98312 | tf_op jit(solution)/shard_map/ppermute | solution.py:23
  76.5 4.3 %collective-permute-start.7 = (bf16[256,6,1,8]{0,3,2,1:T(8,128)(2,1)S(1)}, bf16[256,6,1,8]{0,3,2,1:T(8,128)(2,1)S(1)}, u32[]{:S(2)}, u32[]{:S(2)}) collective-permute-start(bf16[256,6,1,8]{0,3,2,1:T(8,128)(2,1)S(1)} %get-tuple-element.21), channel_id=1, source_target_pairs={{1,0},{3,2},{5,4},{7,6},{9,8},{11,10},{13,12},{15,14},{17,16},{19,... | collective-permute-start | bytes 73736 | tf_op jit(solution)/shard_map/ppermute | solution.py:25
  77.8 3.9 %collective-permute-start.6 = (bf16[256,6,1,8]{0,3,2,1:T(8,128)(2,1)S(1)}, bf16[256,6,1,8]{0,3,2,1:T(8,128)(2,1)S(1)}, u32[]{:S(2)}, u32[]{:S(2)}) collective-permute-start(bf16[256,6,1,8]{0,3,2,1:T(8,128)(2,1)S(1)} %get-tuple-element.20), channel_id=1, source_target_pairs={{0,1},{2,3},{4,5},{6,7},{8,9},{10,11},{12,13},{14,15},{16,17},{18,... | collective-permute-start | bytes 73736 | tf_op jit(solution)/shard_map/ppermute | solution.py:23
  82.9 0.9 copy-start.1
  92.7 3.1 %copy-start.3 = (bf16[256,4,64]{0,2,1:T(8,128)(2,1)S(1)}, bf16[256,4,64]{0,2,1:T(8,128)(2,1)}, u32[]{:S(2)}) copy-start(bf16[256,4,64]{0,2,1:T(8,128)(2,1)} %param.4) | copy-start | bytes 393220
Sparse Core Ops, SparseCore 0:
  11.3 20.4 all-gather.4
  33.5 19.2 all-gather.2
  66.9 18.0 reduce-scatter.4
  92.9 18.5 reduce-scatter.6

commit v2 on v1

v2 whole, which is shorter than its diff:
```python
import functools
import math

import jax
import jax.numpy as jnp
from jax import lax
from jax.experimental import pallas as pl
from jax.experimental.pallas import tpu as pltpu
from jax.sharding import PartitionSpec as P

CH = 256
HALF = 128
TAPS = 27
RAD = 16
AXIAL = 8
AZ_DEV = 4
ROWS = RAD * AXIAL
OWN_ROWS = ROWS // 2
CELLS_CHIP = AZ_DEV * ROWS

NX, NY, NZ = 4, 4, 8
EXTENT = {"x": NX, "y": NY, "z": NZ}
TAP_LANES = 128
PARTS = (
    ("z", "y", "x", 0, 5, True),
    ("z", "y", "x", 5, 4, False),
    ("x", "z", "y", 9, 5, True),
    ("x", "z", "y", 14, 4, False),
    ("y", "z", "x", 18, 5, True),
    ("y", "z", "x", 23, 4, False),
)


def chain_lengths(axis, longer_below):
    count = EXTENT[axis]
    longer, shorter = count // 2, count - 1 - count // 2
    return (longer, shorter) if longer_below else (shorter, longer)


def chunk_shape(axes_done, axis, taps):
    rows = 16 if "z" in axes_done + (axis,) else 128
    lead = () if ("x" in axes_done + (axis,) or "y" in axes_done + (axis,)) else (4,)
    return lead + (rows, taps * TAP_LANES)


class Links:
    def __init__(self, send_sems, recv_sems):
        self.send_sems, self.recv_sems, self.used, self.started = send_sems, recv_sems, 0, []
        flat = lax.axis_index("az")
        self.flat, self.core = flat, lax.axis_index("grp")
        self.at = {"x": flat % NX, "y": (flat // NX) % NY, "z": flat // (NX * NY)}

    def index(self, axis, shift):
        return (self.at[axis] + (shift + EXTENT[axis])) % EXTENT[axis]

    def peer(self, axis, shift):
        to = dict(self.at)
        to[axis] = self.index(axis, shift)
        return {"az": (to["z"] * NY + to["y"]) * NX + to["x"], "grp": self.core}

    def beside(self, shift, core):
        count = NX * NY * NZ
        return {"az": (self.flat + (shift + count)) % count, "grp": core}

    def copy(self, source, target, axis, shift):
        return self.send(source, target, self.peer(axis, shift))

    def send(self, source, target, device):
        number = self.used
        self.used += 1
        handle = pltpu.make_async_remote_copy(
            src_ref=source,
            dst_ref=target,
            send_sem=self.send_sems.at[number],
            recv_sem=self.recv_sems.at[number],
            device_id=device,
            device_id_type=pl.DeviceIdType.MESH,
        )
        handle.start()
        self.started.append(handle)
        return handle


def piece(ref, axes, at, lanes):
    rows = pl.ds(0, 128)
    if "z" in axes:
        rows = pl.ds(pl.multiple_of(at["z"] * 16, 16), 16)
    lead = [a for a in axes if a != "z"]
    first = at[lead[0]] if lead else slice(None)
    return ref.at[first, rows, lanes]


def scatter_axis(links, axis, longer_below, own, buffers):
    below, above = chain_lengths(axis, longer_below)
    ways = [(1, below, buffers[0], buffers[1]), (-1, above, buffers[2], buffers[3])]
    last = {}
    for step in range(1, max(below, above) + 1):
        for sense, length, stage, landing in ways:
            if step > length:
                continue
            total = own(links.index(axis, sense * (length - step + 1)))
            if step > 1:
                last[sense].wait_recv()
                total = total + landing[step - 2].astype(jnp.float32)
            stage[step - 1] = total.astype(jnp.bfloat16)
            last[sense] = links.copy(stage.at[step - 1], landing.at[step - 1], axis, sense)
        yield
    total = own(links.at[axis])
    for sense, length, stage, landing in ways:
        last[sense].wait_recv()
        total = total + landing[length - 1].astype(jnp.float32)
    return total


def gather_axis(links, axis, longer_below, view):
    below, above = chain_lengths(axis, longer_below)
    last = {}
    for step in range(1, max(below, above) + 1):
        for sense, length in ((1, below), (-1, above)):
            if step > length:
                continue
            if step > 1:
                last[sense].wait_recv()
            chunk = view(links.index(axis, -sense * (step - 1)))
            last[sense] = links.copy(chunk, chunk, axis, sense)
        yield
    for sense in (1, -1):
        last[sense].wait_recv()


def reduce_part(links, part, source, result, buffers):
    first, second, third, tap, taps, longer_below = part
    lanes = pl.ds(tap * TAP_LANES, taps * TAP_LANES)
    one, two, three = buffers[:5], buffers[5:10], buffers[10:]

    def own_first(index):
        return piece(source, (first,), {first: index}, lanes)[...].astype(jnp.float32)

    total = yield from scatter_axis(links, first, longer_below, own_first, one[:4])
    one[4][...] = total

    def own_second(index):
        if second == "z":
            return one[4][pl.ds(pl.multiple_of(index * 16, 16), 16), :]
        return one[4][index]

    total = yield from scatter_axis(links, second, not longer_below, own_second, two[:4])
    mine, landing = three
    landing[links.at[third]] = total.astype(jnp.bfloat16)
    handles = [
        links.copy(landing.at[links.at[third]], landing.at[links.at[third]], third, shift)
        for shift in (1, -1, 2)
    ]
    yield
    for handle in handles:
        handle.wait_recv()
    total = landing[0].astype(jnp.float32)
    for index in range(1, EXTENT[third]):
        total = total + landing[index].astype(jnp.float32)
    piece(result, (first, second), links.at, lanes)[...] = total.astype(jnp.bfloat16)
    at = links.at
    yield from gather_axis(
        links,
        second,
        longer_below,
        lambda index: piece(result, (first, second), {**at, second: index}, lanes),
    )
    yield from gather_axis(
        links,
        first,
        not longer_below,
        lambda index: piece(result, (first,), {**at, first: index}, lanes),
    )


def part_scratch(part):
    first, second, third, tap, taps, longer_below = part
    shapes = []
    one = chunk_shape((), first, taps)
    two = chunk_shape((first,), second, taps)
    for axis, shape, flag in ((first, one, longer_below), (second, two, not longer_below)):
        below, above = chain_lengths(axis, flag)
        for length in (below, below, above, above):
            shapes.append(pltpu.VMEM((length,) + shape, jnp.bfloat16))
        shapes.append(pltpu.VMEM(shape, jnp.float32))
    shapes.append(pltpu.VMEM((8, 128), jnp.float32))
    shapes.append(pltpu.VMEM((EXTENT[third],) + two, jnp.bfloat16))
    return shapes


def greet(links):
    barrier = pltpu.get_barrier_semaphore()
    peers = [links.peer("z", 1), links.peer("z", -1), links.beside(0, 1 - links.core)]
    peers += [links.peer(axis, shift) for axis in "xy" for shift in (1, -1, 2)]
    peers += [
        links.beside(shift, core) for shift in (1, -1) for core in (links.core, 1 - links.core)
    ]
    for device in peers:
        pl.semaphore_signal(
            barrier, inc=1, device_id=device, device_id_type=pl.DeviceIdType.MESH
        )
    pl.semaphore_wait(barrier, len(peers))


def shifted_copies(level, padded):
    channels = level.shape[3]
    along = lax.broadcasted_iota(jnp.int32, (RAD, AXIAL, channels), 1)
    rim = jnp.zeros((AXIAL, channels), jnp.bfloat16).astype(jnp.float32)

    def one_slab(slab, carry):
        here = level[1, slab].astype(jnp.float32).reshape(RAD, AXIAL, channels)
        below = jnp.where(along == 0, 0.0, pltpu.roll(here, 1, 1))
        above = jnp.where(along == AXIAL - 1, 0.0, pltpu.roll(here, AXIAL - 1, 1))
        for offset, values in ((0, below), (1, here), (2, above)):
            rows = values.reshape(ROWS, channels)
            if offset != 1:
                level[offset, slab] = rows.astype(jnp.bfloat16)
            padded[offset, slab] = jnp.concatenate((rim, rows, rim), axis=0).astype(jnp.bfloat16)
        return carry

    lax.fori_loop(0, AZ_DEV + 2, one_slab, 0)


def window(level, padded, along_az, along_rad, along_ax):
    channels = level.shape[3]
    slabs = pl.ds(along_az, AZ_DEV)
    if along_rad == 1:
        picked = level[along_ax, slabs]
    else:
        picked = padded[along_ax, slabs, pl.ds(AXIAL * along_rad, ROWS), :]
    return picked.reshape(CELLS_CHIP, channels)


def tap_lanes(along_az, along_rad, along_ax, width):
    tap = (along_az * 3 + along_rad) * 3 + along_ax
    return pl.ds(pl.multiple_of(tap * width, width), width)


def convolve(level, padded, weight, total):
    total[...] = jnp.zeros_like(total)

    def one_step(step, carry):
        along_az, along_ax = step // 3, step % 3
        added = total[...]
        for along_rad in range(3):
            added = added + lax.dot_general(
                window(level, padded, along_az, along_rad, along_ax),
                weight[:, tap_lanes(along_az, along_rad, along_ax, CH)],
                (((1,), (1,)), ((), ())),
                preferred_element_type=jnp.float32,
            )
        total[...] = added
        return carry

    lax.fori_loop(0, 9, one_step, 0)


def convolve_back(level, padded, weight, total):
    total[...] = jnp.zeros_like(total)

    def one_step(step, carry):
        along_az, along_ax = step // 3, step % 3
        columns = jnp.concatenate(
            [window(level, padded, 2 - along_az, 2 - rad, 2 - along_ax) for rad in range(3)], axis=1
        )
        rows = jnp.concatenate(
            [weight[:, tap_lanes(along_az, rad, along_ax, CH)] for rad in range(3)], axis=0
        )
        update = jnp.dot(columns, rows, preferred_element_type=jnp.float32)
        for side in range(2):
            total[side] = total[side] + update[:, side * HALF : (side + 1) * HALF]
        return carry

    lax.fori_loop(0, 9, one_step, 0)


def weight_terms(turned, level, padded, terms, which, along_az):
    def one_step(along_ax, carry):
        for along_rad in range(3):
            update = jnp.dot(
                turned[...],
                window(level, padded, along_az, along_rad, along_ax),
                preferred_element_type=jnp.float32,
            )
            lanes = tap_lanes(along_az, along_rad, along_ax, HALF)
            for side in range(2):
                terms[2 * which + side, :, lanes] = update[:, side * HALF : (side + 1) * HALF]
        return carry

    lax.fori_loop(0, 3, one_step, 0)


def flow_part(links, features, level, padded, weight, total, mine, flow):
    core = links.core
    lanes = pl.ds(pl.multiple_of(core * HALF, HALF), HALF)
    convolve(level, padded, weight, total)
    yield
    own = features[1, pl.ds(1, AZ_DEV), :, lanes].astype(jnp.float32)
    mine[...] = (own + total[...].reshape(AZ_DEV, ROWS, HALF)).astype(jnp.bfloat16)
    here = pl.ds(pl.multiple_of(core * OWN_ROWS, OWN_ROWS), OWN_ROWS)
    there = pl.ds(pl.multiple_of((1 - core) * OWN_ROWS, OWN_ROWS), OWN_ROWS)
    flow[:, :, lanes] = mine[:, here, :]
    handle = links.send(mine.at[:, there, :], flow.at[:, :, lanes], links.beside(0, 1 - core))
    yield
    handle.wait_recv()


def exchange_rims(links, source, target, rows):
    core = links.core
    handles = []
    for to in (1 - core, core):
        for shift, slab, landing in ((1, AZ_DEV - 1, 0), (-1, 0, AZ_DEV + 1)):
            given, taken = source(slab, to), target(landing, to)
            handles.append(links.send(given, taken, links.beside(shift, to)))
        if to is not core:
            handles.append(
                links.send(
                    source(slice(None), to), target(pl.ds(1, AZ_DEV), to), links.beside(0, to)
                )
            )
    return handles


def whole_kernel(
    features,
    cotangent,
    w_first,
    w_second,
    flow,
    result,
    send_sems,
    recv_sems,
    local_sems,
    first_rows,
    second_rows,
    in_level,
    in_padded,
    cot_level,
    cot_padded,
    hid_level,
    hid_padded,
    pre,
    second,
    back,
    back_other,
    turned,
    mine,
    terms,
    *buffers,
):
    links = Links(send_sems, recv_sems)
    core = links.core
    here = pl.ds(pl.multiple_of(core * OWN_ROWS, OWN_ROWS), OWN_ROWS)
    cells = pl.ds(1, AZ_DEV)

    def lanes(which):
        return pl.ds(pl.multiple_of(which * HALF, HALF), HALF)

    loads = [
        pltpu.make_async_copy(*pair, local_sems.at[number])
        for number, pair in enumerate(
            (
                (features, in_level.at[1, cells, here, :]),
                (cotangent.at[:, :, lanes(core)], cot_level.at[1, cells, here, :]),
                (w_first, first_rows),
                (w_second, second_rows),
            )
        )
    ]
    for load in loads:
        load.start()
    greet(links)
    field_in = exchange_rims(
        links,
        lambda slab, to: features.at[slab],
        lambda slab, to: in_level.at[1, slab, here, :],
        here,
    )
    field_cot = exchange_rims(
        links,
        lambda slab, to: cotangent.at[slab, :, lanes(to)],
        lambda slab, to: cot_level.at[1, slab, here, :],
        here,
    )
    loads[0].wait()
    loads[2].wait()
    for handle in field_in:
        handle.wait_recv()
    shifted_copies(in_level, in_padded)
    convolve(in_level, in_padded, first_rows, pre)
    values = pre[...]
    hidden = values * jax.nn.sigmoid(values)
    hid_level[1, cells, :, lanes(core)] = hidden.astype(jnp.bfloat16).reshape(AZ_DEV, ROWS, HALF)
    field_hid = exchange_rims(
        links,
        lambda slab, to: hid_level.at[
            1, pl.ds(1, AZ_DEV) if isinstance(slab, slice) else slab + 1, :, lanes(core)
        ],
        lambda slab, to: hid_level.at[1, slab, :, lanes(core)],
        here,
    )
    loads[1].wait()
    loads[3].wait()
    for handle in field_cot:
        handle.wait_recv()
    shifted_copies(cot_level, cot_padded)
    convolve_back(cot_level, cot_padded, second_rows, back)
    swap = links.send(back.at[1 - core], back_other, links.beside(0, 1 - core))
    own_cot = cot_level[1, cells].reshape(CELLS_CHIP, HALF).astype(jnp.float32)
    turned[1] = own_cot.T.astype(jnp.bfloat16)
    swap.wait_recv()
    values = pre[...]
    sigma = jax.nn.sigmoid(values)
    slope = (back[core] + back_other[...]) * (sigma * (1.0 + values * (1.0 - sigma)))
    turned[0] = slope.T.astype(jnp.bfloat16)
    for along_az in range(3):
        weight_terms(turned.at[0], in_level, in_padded, terms, 0, along_az)
    for handle in field_hid:
        handle.wait_recv()
    shifted_copies(hid_level, hid_padded)
    running, used = [], 0

    def advance():
        for one in list(running):
            try:
                next(one)
            except StopIteration:
                running.remove(one)

    for number, part in enumerate(PARTS):
        if part[3] % 9 == 0:
            weight_terms(turned.at[1], hid_level, hid_padded, terms, 1, part[3] // 9)
            advance()
        count = len(part_scratch(part))
        running.append(reduce_part(links, part, terms, result, buffers[used : used + count]))
        used += count
        next(running[-1])
    running.append(
        flow_part(links, in_level, hid_level, hid_padded, second_rows, second, mine, flow)
    )
    while running:
        advance()
    for handle in links.started:
        handle.wait_send()


COPIES = 192


def whole_layer(features, cotangent, w_first, w_second):
    field = (3, AZ_DEV + 2, ROWS)
    padded = (3, AZ_DEV + 2, ROWS + 2 * AXIAL)
    scratch = [
        pltpu.SemaphoreType.DMA((COPIES,)),
        pltpu.SemaphoreType.DMA((COPIES,)),
        pltpu.SemaphoreType.DMA((4,)),
        pltpu.VMEM((HALF, TAPS * CH), jnp.bfloat16),
        pltpu.VMEM((HALF, TAPS * CH), jnp.bfloat16),
        pltpu.VMEM(field + (CH,), jnp.bfloat16),
        pltpu.VMEM(padded + (CH,), jnp.bfloat16),
        pltpu.VMEM(field + (HALF,), jnp.bfloat16),
        pltpu.VMEM(padded + (HALF,), jnp.bfloat16),
        pltpu.VMEM(field + (CH,), jnp.bfloat16),
        pltpu.VMEM(padded + (CH,), jnp.bfloat16),
        pltpu.VMEM((CELLS_CHIP, HALF), jnp.float32),
        pltpu.VMEM((CELLS_CHIP, HALF), jnp.float32),
        pltpu.VMEM((2, CELLS_CHIP, HALF), jnp.float32),
        pltpu.VMEM((CELLS_CHIP, HALF), jnp.float32),
        pltpu.VMEM((2, HALF, CELLS_CHIP), jnp.bfloat16),
        pltpu.VMEM((AZ_DEV, ROWS, HALF), jnp.bfloat16),
        pltpu.VMEM((4, HALF, TAPS * HALF), jnp.float32),
    ]
    for part in PARTS:
        scratch += part_scratch(part)
    return pl.pallas_call(
        whole_kernel,
        out_shape=(
            jax.ShapeDtypeStruct((AZ_DEV, OWN_ROWS, CH), jnp.bfloat16),
            jax.ShapeDtypeStruct((4, HALF, TAPS * HALF), jnp.bfloat16),
        ),
        in_specs=[pl.BlockSpec(memory_space=pl.ANY)] * 4,
        out_specs=(pl.BlockSpec(memory_space=pltpu.VMEM), pl.BlockSpec(memory_space=pltpu.VMEM)),
        scratch_shapes=scratch,
        compiler_params=pltpu.CompilerParams(
            collective_id=0, has_side_effects=True, vmem_limit_bytes=56 * 2**20
        ),
        name="both_layers",
    )(features, cotangent, w_first, w_second)


def widen_kernel(factor, summed, grad_first, grad_second):
    def put(target):
        for tap in range(9):
            for side in range(2):
                target[:, (2 * tap + side) * HALF : (2 * tap + side + 1) * HALF] = (
                    summed[side, :, tap * HALF : (tap + 1) * HALF].astype(jnp.float32) * factor
                )

    @pl.when(pl.program_id(0) == 0)
    def _():
        put(grad_first)

    @pl.when(pl.program_id(0) == 1)
    def _():
        put(grad_second)


def widen(summed, factor):
    third = TAPS * CH // 3
    shape = jax.ShapeDtypeStruct((HALF, TAPS * CH), jnp.float32)
    return pl.pallas_call(
        functools.partial(widen_kernel, factor),
        grid=(2, 3),
        out_shape=(shape, shape),
        in_specs=[pl.BlockSpec((2, HALF, third // 2), lambda g, p: (g, 0, p))],
        out_specs=(
            pl.BlockSpec((HALF, third), lambda g, p: (0, jnp.where(g == 0, p, 2))),
            pl.BlockSpec((HALF, third), lambda g, p: (0, jnp.where(g == 0, 0, p))),
        ),
        compiler_params=pltpu.CompilerParams(vmem_limit_bytes=24 * 2**20),
        name="widen",
    )(summed)


def local(features, cotangent, w_first, w_second):
    factor = 1.0 / math.sqrt(NX * NY * NZ * CELLS_CHIP)
    flow, summed = whole_layer(
        features.transpose(1, 2, 0), cotangent.transpose(1, 2, 0), w_first, w_second
    )
    grad_first, grad_second = widen(summed, factor)
    return (flow.transpose(2, 0, 1), grad_first, grad_second)


def solution(mesh):
    in_specs = (P(None, "az", "grp"), P(None, "az", "grp"), P("grp", None), P("grp", None))
    out_specs = (P(None, "az", "grp"), P("grp", None), P("grp", None))
    return jax.shard_map(local, mesh=mesh, in_specs=in_specs, out_specs=out_specs, check_vma=False)
```

time: 225 us -> 114 us (0.51)
  local copies, waits for them, and re-layouts: 59.3 us -> 2.65 us
  Pallas kernels: 66.7 us -> 110 us
  waiting for transfers between devices: 34.7 us -> 0 us
  starting transfers between devices: 22.8 us -> 0 us
  matrix products: 19.9 us -> 0 us
  between operations: 14.7 us -> 0.65 us
  other arithmetic: 5.6 us -> 0 us
    pallas_call x1 -> x2, Pallas kernels: 66.7 us -> 110 us  [the longest x1 106 us: whole_layer(): pl.pallas_call(whole_kernel, out_shape=(jax.ShapeDtypeStruct((AZ_DEV, OWN...]
    unnamed x89 -> x5, local copies, waits for them, and re-layouts: 28.5 us -> 2.65 us
    ppermute x12 -> x0, starting transfers between devices: 22.6 us -> none  [the longest x6 13.6 us: with_halo(): lax.ppermute(head, axis, [((i + 1) % count, i) for i in range(ends)])]
    dot_general x4 -> x0, matrix products: 19.9 us -> none  [the longest x2 11.9 us: contract_cells(): lax.dot_general(left, right, (((1,), (1,)), ((), ())), preferred_element_...]
    all_gather x2 -> x0, waiting for transfers between devices: 13.9 us -> none  [rows_forward(): lax.all_gather(weight, 'grp', axis=0, tiled=True)]
    unnamed x5 -> x0, waiting for transfers between devices: 12.2 us -> none
    ppermute x12 -> x0, waiting for transfers between devices: 8.58 us -> none  [the longest x6 6.97 us: with_halo(): lax.ppermute(tail, axis, [(i, (i + 1) % count) for i in range(ends)])]
    mul x1 -> x0, local copies, waits for them, and re-layouts: 8.02 us -> none  [local(): summed = summed.astype(jnp.float32) * factor]
  transfers between devices with their start and end apart: 16 -> 0, of which waited for: 6 -> 0; matrix products, arithmetic and copies ran while one was open for 12% -> 0% of each run, Pallas kernels for 0% -> 0%
where the time goes in v2:
time: 114 us; the launch traced here: 113 us
  Pallas kernels  110 us (96%)
  local copies, waits for them, and re-layouts  2.65 us (2%)
    pallas_call x1, Pallas kernels, whole_layer(): pl.pallas_call(whole_kernel, out_shape=(jax.ShapeDtypeStruct((AZ_DEV, OWN...  106 us
    pallas_call x1, Pallas kernels, widen(): pl.pallas_call(functools.partial(widen_kernel, factor), grid=(2, 3), out_...  4.25 us
    unnamed x5, local copies, waits for them, and re-layouts  2.65 us

profile of v2, /device:TPU:8, one launch (start us, length us, event | category | flops | bytes accessed | tf_op | source)
XLA Modules:
  0.0 113.5 jit_solution(15711952806540023844)
XLA Ops:
  0.6 105.9 %both_layers.1 = (bf16[4,64,256]{2,1,0:T(8,128)(2,1)}, bf16[4,128,3456]{2,1,0:T(8,128)(2,1)}) custom-call(bf16[4,64,256]{2,1,0:T(8,128)(2,1)} %bitcast.4, bf16[4,64,256]{2,1,0:T(8,128)(2,1)} %bitcast.5, bf16[128,6912]{1,0:T(8,128)(2,1)} %w_first.1, bf16[128,6912]{1,0:T(8,128)(2,1)} %w_second.1), custom_call_target="tpu_custom_call" | custom-call | tf_op jit(solution)/shard_map/both_layers/pallas_call | solution.py:475
  106.6 0.0 copy-start
  106.6 2.0 %copy-done = bf16[4,128,3456]{2,1,0:T(8,128)(2,1)S(1)} copy-done((bf16[4,128,3456]{2,1,0:T(8,128)(2,1)S(1)}, bf16[4,128,3456]{2,1,0:T(8,128)(2,1)}, u32[]{:S(2)}) %copy-start) | copy-done | bytes 3538968
  108.6 0.0 copy-start.1
  108.6 4.2 %widen.1 = (f32[128,6912]{1,0:T(8,128)}, f32[128,6912]{1,0:T(8,128)}) custom-call(bf16[4,128,3456]{2,1,0:T(8,128)(2,1)S(1)} %copy-done), custom_call_target="tpu_custom_call" | custom-call | tf_op jit(solution)/shard_map/widen/pallas_call | solution.py:511
  112.8 0.0 copy-done.1
  112.8 0.7 copy.8
Async XLA Ops:
  106.6 2.0 %copy-start = (bf16[4,128,3456]{2,1,0:T(8,128)(2,1)S(1)}, bf16[4,128,3456]{2,1,0:T(8,128)(2,1)}, u32[]{:S(2)}) copy-start(bf16[4,128,3456]{2,1,0:T(8,128)(2,1)} %get-tuple-element.8.summed) | copy-start | bytes 10616836
  108.6 4.3 %copy-start.1 = (bf16[4,64,256]{2,1,0:T(8,128)(2,1)S(1)}, bf16[4,64,256]{2,1,0:T(8,128)(2,1)}, u32[]{:S(2)}) copy-start(bf16[4,64,256]{2,1,0:T(8,128)(2,1)} %get-tuple-element.7) | copy-start | bytes 393220

commit v3 on v2

--- a/solution.py
+++ b/solution.py
@@ -22,30 +22,23 @@
 EXTENT = {"x": NX, "y": NY, "z": NZ}
 TAP_LANES = 128
 PARTS = (
-    ("z", "y", "x", 0, 5, True),
-    ("z", "y", "x", 5, 4, False),
-    ("x", "z", "y", 9, 5, True),
-    ("x", "z", "y", 14, 4, False),
-    ("y", "z", "x", 18, 5, True),
-    ("y", "z", "x", 23, 4, False),
+    ("x", "y", 0, 5, 1),
+    ("y", "x", 5, 4, 1),
+    ("y", "x", 9, 5, -1),
+    ("x", "y", 14, 4, -1),
+    ("x", "y", 18, 5, 1),
+    ("y", "x", 23, 4, 1),
 )
 
 
-def chain_lengths(axis, longer_below):
-    count = EXTENT[axis]
-    longer, shorter = count // 2, count - 1 - count // 2
-    return (longer, shorter) if longer_below else (shorter, longer)
-
-
-def chunk_shape(axes_done, axis, taps):
-    rows = 16 if "z" in axes_done + (axis,) else 128
-    lead = () if ("x" in axes_done + (axis,) or "y" in axes_done + (axis,)) else (4,)
-    return lead + (rows, taps * TAP_LANES)
+BYTES_PER_US = 65000.0
+SEND_US, HOP_US, STEP_US, CONVOLVE_US = 1.5, 0.3, 0.15, 0.45
 
 
 class Links:
     def __init__(self, send_sems, recv_sems):
         self.send_sems, self.recv_sems, self.used, self.started = send_sems, recv_sems, 0, []
+        self.now, self.busy = 0.0, {}
         flat = lax.axis_index("az")
         self.flat, self.core = flat, lax.axis_index("grp")
         self.at = {"x": flat % NX, "y": (flat // NX) % NY, "z": flat // (NX * NY)}
@@ -63,7 +56,11 @@
         return {"az": (self.flat + (shift + count)) % count, "grp": core}
 
     def copy(self, source, target, axis, shift):
-        return self.send(source, target, self.peer(axis, shift))
+        lane, hops = (axis, shift > 0), abs(shift)
+        begin = max(self.now, self.busy.get(lane, 0.0))
+        self.busy[lane] = begin + hops * 2 * math.prod(source.shape) / BYTES_PER_US
+        handle = self.send(source, target, self.peer(axis, shift))
+        return handle, self.busy[lane] + SEND_US + HOP_US * hops
 
     def send(self, source, target, device):
         number = self.used
@@ -90,107 +87,116 @@
     return ref.at[first, rows, lanes]
 
 
-def scatter_axis(links, axis, longer_below, own, buffers):
-    below, above = chain_lengths(axis, longer_below)
-    ways = [(1, below, buffers[0], buffers[1]), (-1, above, buffers[2], buffers[3])]
-    last = {}
-    for step in range(1, max(below, above) + 1):
-        for sense, length, stage, landing in ways:
-            if step > length:
-                continue
-            total = own(links.index(axis, sense * (length - step + 1)))
-            if step > 1:
-                last[sense].wait_recv()
-                total = total + landing[step - 2].astype(jnp.float32)
-            stage[step - 1] = total.astype(jnp.bfloat16)
-            last[sense] = links.copy(stage.at[step - 1], landing.at[step - 1], axis, sense)
-        yield
+ROUTES = {4: ((2, 1), (-1, -1)), 8: ((4, 1), (2, 1), (-3, -1), (-1, -1))}
+
+
+def relays(axis):
+    return [(owner - stop, stop) for owner, stop in ROUTES[EXTENT[axis]] if owner != stop]
+
+
+def arrivals(axis):
+    routes = ROUTES[EXTENT[axis]]
+    return [onward for onward, _ in relays(axis)] + [o for o, stop in routes if o == stop]
+
+
+def scatter_axis(links, axis, sense, own, stage, landing):
+    first = []
+    for slot, (owner, stop) in enumerate(ROUTES[EXTENT[axis]]):
+        stage[slot] = own(links.index(axis, sense * owner)).astype(jnp.bfloat16)
+        first.append(links.copy(stage.at[slot], landing.at[slot], axis, sense * stop))
+    last = []
+    slot = len(first)
+    for number, (owner, stop) in enumerate(ROUTES[EXTENT[axis]]):
+        handle, due = first[number]
+        if owner == stop:
+            last.append((number, handle, due))
+            continue
+        onward = owner - stop
+        total = own(links.index(axis, sense * onward))
+        yield due
+        handle.wait_recv()
+        stage[slot] = (total + landing[number].astype(jnp.float32)).astype(jnp.bfloat16)
+        last.append((slot,) + links.copy(stage.at[slot], landing.at[slot], axis, sense * onward))
+        slot += 1
     total = own(links.at[axis])
-    for sense, length, stage, landing in ways:
-        last[sense].wait_recv()
-        total = total + landing[length - 1].astype(jnp.float32)
+    yield max(due for _, _, due in last)
+    for slot, handle, _ in last:
+        handle.wait_recv()
+        total = total + landing[slot].astype(jnp.float32)
     return total
 
 
-def gather_axis(links, axis, longer_below, view):
-    below, above = chain_lengths(axis, longer_below)
-    last = {}
-    for step in range(1, max(below, above) + 1):
-        for sense, length in ((1, below), (-1, above)):
-            if step > length:
-                continue
-            if step > 1:
-                last[sense].wait_recv()
-            chunk = view(links.index(axis, -sense * (step - 1)))
-            last[sense] = links.copy(chunk, chunk, axis, sense)
-        yield
-    for sense in (1, -1):
-        last[sense].wait_recv()
+def gather_axis(links, axis, sense, view):
+    chunk = view(links.at[axis])
+    first = [
+        (onward,) + links.copy(chunk, chunk, axis, sense * onward) for onward in arrivals(axis)
+    ]
+    last = []
+    for number, (onward, stop) in enumerate(relays(axis)):
+        _, handle, due = first[number]
+        yield due
+        handle.wait_recv()
+        chunk = view(links.index(axis, -sense * onward))
+        last.append(links.copy(chunk, chunk, axis, sense * stop))
+    last += [(handle, due) for _, handle, due in first[len(last) :]]
+    yield max(due for _, due in last)
+    for handle, _ in last:
+        handle.wait_recv()
 
 
 def reduce_part(links, part, source, result, buffers):
-    first, second, third, tap, taps, longer_below = part
+    first, third, tap, taps, sense = part
     lanes = pl.ds(tap * TAP_LANES, taps * TAP_LANES)
-    one, two, three = buffers[:5], buffers[5:10], buffers[10:]
+    stage_one, landing_one, sum_one, stage_two, landing_two, landing_three = buffers
 
     def own_first(index):
-        return piece(source, (first,), {first: index}, lanes)[...].astype(jnp.float32)
-
-    total = yield from scatter_axis(links, first, longer_below, own_first, one[:4])
-    one[4][...] = total
+        return source[index, :, lanes]
+
+    sum_one[...] = yield from scatter_axis(
+        links, first, sense, own_first, stage_one, landing_one
+    )
 
     def own_second(index):
-        if second == "z":
-            return one[4][pl.ds(pl.multiple_of(index * 16, 16), 16), :]
-        return one[4][index]
-
-    total = yield from scatter_axis(links, second, not longer_below, own_second, two[:4])
-    mine, landing = three
-    landing[links.at[third]] = total.astype(jnp.bfloat16)
-    handles = [
-        links.copy(landing.at[links.at[third]], landing.at[links.at[third]], third, shift)
-        for shift in (1, -1, 2)
+        return sum_one[pl.ds(pl.multiple_of(index * 16, 16), 16), :]
+
+    total = yield from scatter_axis(links, "z", -sense, own_second, stage_two, landing_two)
+    mine = landing_three.at[links.at[third]]
+    mine[...] = total.astype(jnp.bfloat16)
+    sent = [links.copy(mine, mine, third, shift) for shift in (1, -1, 2)]
+    yield max(due for _, due in sent)
+    for handle, _ in sent:
+        handle.wait_recv()
+    total = landing_three[0].astype(jnp.float32)
+    for index in range(1, EXTENT[third]):
+        total = total + landing_three[index].astype(jnp.float32)
+    at = links.at
+    piece(result, (first, "z"), at, lanes)[...] = total.astype(jnp.bfloat16)
+    yield from gather_axis(
+        links, "z", sense, lambda index: piece(result, (first, "z"), {**at, "z": index}, lanes)
+    )
+    yield from gather_axis(
+        links, first, -sense, lambda index: piece(result, (first,), {first: index}, lanes)
+    )
+
+
+def part_scratch(part):
+    first, third, tap, taps, sense = part
+    one, two = (128, taps * TAP_LANES), (16, taps * TAP_LANES)
+    slots = {axis: EXTENT[axis] - 1 for axis in EXTENT}
+    return [
+        pltpu.VMEM((slots[first],) + one, jnp.bfloat16),
+        pltpu.VMEM((slots[first],) + one, jnp.bfloat16),
+        pltpu.VMEM(one, jnp.float32),
+        pltpu.VMEM((slots["z"],) + two, jnp.bfloat16),
+        pltpu.VMEM((slots["z"],) + two, jnp.bfloat16),
+        pltpu.VMEM((EXTENT[third],) + two, jnp.bfloat16),
     ]
-    yield
-    for handle in handles:
-        handle.wait_recv()
-    total = landing[0].astype(jnp.float32)
-    for index in range(1, EXTENT[third]):
-        total = total + landing[index].astype(jnp.float32)
-    piece(result, (first, second), links.at, lanes)[...] = total.astype(jnp.bfloat16)
-    at = links.at
-    yield from gather_axis(
-        links,
-        second,
-        longer_below,
-        lambda index: piece(result, (first, second), {**at, second: index}, lanes),
-    )
-    yield from gather_axis(
-        links,
-        first,
-        not longer_below,
-        lambda index: piece(result, (first,), {**at, first: index}, lanes),
-    )
-
-
-def part_scratch(part):
-    first, second, third, tap, taps, longer_below = part
-    shapes = []
-    one = chunk_shape((), first, taps)
-    two = chunk_shape((first,), second, taps)
-    for axis, shape, flag in ((first, one, longer_below), (second, two, not longer_below)):
-        below, above = chain_lengths(axis, flag)
-        for length in (below, below, above, above):
-            shapes.append(pltpu.VMEM((length,) + shape, jnp.bfloat16))
-        shapes.append(pltpu.VMEM(shape, jnp.float32))
-    shapes.append(pltpu.VMEM((8, 128), jnp.float32))
-    shapes.append(pltpu.VMEM((EXTENT[third],) + two, jnp.bfloat16))
-    return shapes
 
 
 def greet(links):
     barrier = pltpu.get_barrier_semaphore()
-    peers = [links.peer("z", 1), links.peer("z", -1), links.beside(0, 1 - links.core)]
+    peers = [links.peer("z", shift) for shift in (1, -1, 2, -2, 3, -3)]
+    peers += [links.beside(0, 1 - links.core)]
     peers += [links.peer(axis, shift) for axis in "xy" for shift in (1, -1, 2)]
     peers += [
         links.beside(shift, core) for shift in (1, -1) for core in (links.core, 1 - links.core)
@@ -233,23 +239,27 @@
 
 def tap_lanes(along_az, along_rad, along_ax, width):
     tap = (along_az * 3 + along_rad) * 3 + along_ax
-    return pl.ds(pl.multiple_of(tap * width, width), width)
+    start = tap * width
+    return pl.ds(start if isinstance(tap, int) else pl.multiple_of(start, width), width)
+
+
+def convolve_step(level, padded, weight, total, along_az, along_ax):
+    added = total[...]
+    for along_rad in range(3):
+        added = added + lax.dot_general(
+            window(level, padded, along_az, along_rad, along_ax),
+            weight[:, tap_lanes(along_az, along_rad, along_ax, CH)],
+            (((1,), (1,)), ((), ())),
+            preferred_element_type=jnp.float32,
+        )
+    total[...] = added
 
 
 def convolve(level, padded, weight, total):
     total[...] = jnp.zeros_like(total)
 
     def one_step(step, carry):
-        along_az, along_ax = step // 3, step % 3
-        added = total[...]
-        for along_rad in range(3):
-            added = added + lax.dot_general(
-                window(level, padded, along_az, along_rad, along_ax),
-                weight[:, tap_lanes(along_az, along_rad, along_ax, CH)],
-                (((1,), (1,)), ((), ())),
-                preferred_element_type=jnp.float32,
-            )
-        total[...] = added
+        convolve_step(level, padded, weight, total, step // 3, step % 3)
         return carry
 
     lax.fori_loop(0, 9, one_step, 0)
@@ -293,15 +303,18 @@
 def flow_part(links, features, level, padded, weight, total, mine, flow):
     core = links.core
     lanes = pl.ds(pl.multiple_of(core * HALF, HALF), HALF)
-    convolve(level, padded, weight, total)
-    yield
+    total[...] = jnp.zeros_like(total)
+    for step in range(9):
+        yield None
+        convolve_step(level, padded, weight, total, step // 3, step % 3)
+        links.now += CONVOLVE_US
     own = features[1, pl.ds(1, AZ_DEV), :, lanes].astype(jnp.float32)
     mine[...] = (own + total[...].reshape(AZ_DEV, ROWS, HALF)).astype(jnp.bfloat16)
     here = pl.ds(pl.multiple_of(core * OWN_ROWS, OWN_ROWS), OWN_ROWS)
     there = pl.ds(pl.multiple_of((1 - core) * OWN_ROWS, OWN_ROWS), OWN_ROWS)
     flow[:, :, lanes] = mine[:, here, :]
     handle = links.send(mine.at[:, there, :], flow.at[:, :, lanes], links.beside(0, 1 - core))
-    yield
+    yield links.now + 60.0
     handle.wait_recv()
 
 
@@ -418,28 +431,29 @@
     for handle in field_hid:
         handle.wait_recv()
     shifted_copies(hid_level, hid_padded)
-    running, used = [], 0
-
-    def advance():
-        for one in list(running):
-            try:
-                next(one)
-            except StopIteration:
-                running.remove(one)
-
-    for number, part in enumerate(PARTS):
-        if part[3] % 9 == 0:
-            weight_terms(turned.at[1], hid_level, hid_padded, terms, 1, part[3] // 9)
-            advance()
+    waiting, used = [], 0
+
+    def advance(one):
+        links.now += STEP_US
+        try:
+            waiting.append((next(one), one))
+        except StopIteration:
+            pass
+
+    for part in PARTS:
+        if part[2] % 9 == 0:
+            weight_terms(turned.at[1], hid_level, hid_padded, terms, 1, part[2] // 9)
+            links.now += 1.0
         count = len(part_scratch(part))
-        running.append(reduce_part(links, part, terms, result, buffers[used : used + count]))
+        advance(reduce_part(links, part, terms, result, buffers[used : used + count]))
         used += count
-        next(running[-1])
-    running.append(
-        flow_part(links, in_level, hid_level, hid_padded, second_rows, second, mine, flow)
-    )
-    while running:
-        advance()
+    advance(flow_part(links, in_level, hid_level, hid_padded, second_rows, second, mine, flow))
+    while waiting:
+        due = [links.now + CONVOLVE_US if at is None else at for at, _ in waiting]
+        soonest = min(range(len(due)), key=due.__getitem__)
+        at, one = waiting.pop(soonest)
+        links.now = max(links.now, at or 0.0)
+        advance(one)
     for handle in links.started:
         handle.wait_send()
 

time: 114 us -> 97.5 us (0.86); the launches traced: 113 us -> 95.7 us
  Pallas kernels: 110 us -> 92.4 us
    pallas_call x1, Pallas kernels: 106 us -> 88.2 us  [whole_layer(): pl.pallas_call(whole_kernel, out_shape=(jax.ShapeDtypeStruct((AZ_DEV, OWN...]
where the time goes in v3:
time: 97.5 us; the launch traced here: 95.7 us
  Pallas kernels  92.4 us (95%)
  local copies, waits for them, and re-layouts  2.65 us (3%)
    pallas_call x1, Pallas kernels, whole_layer(): pl.pallas_call(whole_kernel, out_shape=(jax.ShapeDtypeStruct((AZ_DEV, OWN...  88.2 us
    pallas_call x1, Pallas kernels, widen(): pl.pallas_call(functools.partial(widen_kernel, factor), grid=(2, 3), out_...  4.25 us
    unnamed x5, local copies, waits for them, and re-layouts  2.65 us

profile of v3, /device:TPU:8, one launch (start us, length us, event | category | flops | bytes accessed | tf_op | source)
XLA Modules:
  0.0 95.7 jit_solution(7964049834486794043)
XLA Ops:
  0.6 88.2 %both_layers.1 = (bf16[4,64,256]{2,1,0:T(8,128)(2,1)}, bf16[4,128,3456]{2,1,0:T(8,128)(2,1)}) custom-call(bf16[4,64,256]{2,1,0:T(8,128)(2,1)} %bitcast.4, bf16[4,64,256]{2,1,0:T(8,128)(2,1)} %bitcast.5, bf16[128,6912]{1,0:T(8,128)(2,1)} %w_first.1, bf16[128,6912]{1,0:T(8,128)(2,1)} %w_second.1), custom_call_target="tpu_custom_call" | custom-call | tf_op jit(solution)/shard_map/both_layers/pallas_call | solution.py:489
  88.8 0.0 copy-start
  88.8 2.0 %copy-done = bf16[4,128,3456]{2,1,0:T(8,128)(2,1)S(1)} copy-done((bf16[4,128,3456]{2,1,0:T(8,128)(2,1)S(1)}, bf16[4,128,3456]{2,1,0:T(8,128)(2,1)}, u32[]{:S(2)}) %copy-start) | copy-done | bytes 3538968
  90.8 0.0 copy-start.1
  90.8 4.2 %widen.1 = (f32[128,6912]{1,0:T(8,128)}, f32[128,6912]{1,0:T(8,128)}) custom-call(bf16[4,128,3456]{2,1,0:T(8,128)(2,1)S(1)} %copy-done), custom_call_target="tpu_custom_call" | custom-call | tf_op jit(solution)/shard_map/widen/pallas_call | solution.py:525
  95.1 0.0 copy-done.1
  95.1 0.7 copy.8
Async XLA Ops:
  88.8 2.0 %copy-start = (bf16[4,128,3456]{2,1,0:T(8,128)(2,1)S(1)}, bf16[4,128,3456]{2,1,0:T(8,128)(2,1)}, u32[]{:S(2)}) copy-start(bf16[4,128,3456]{2,1,0:T(8,128)(2,1)} %get-tuple-element.8.summed) | copy-start | bytes 10616836
  90.8 4.3 %copy-start.1 = (bf16[4,64,256]{2,1,0:T(8,128)(2,1)S(1)}, bf16[4,64,256]{2,1,0:T(8,128)(2,1)}, u32[]{:S(2)}) copy-start(bf16[4,64,256]{2,1,0:T(8,128)(2,1)} %get-tuple-element.7) | copy-start | bytes 393220

commit v4 on v3

--- a/solution.py
+++ b/solution.py
@@ -22,17 +22,22 @@
 EXTENT = {"x": NX, "y": NY, "z": NZ}
 TAP_LANES = 128
 PARTS = (
-    ("x", "y", 0, 5, 1),
-    ("y", "x", 5, 4, 1),
-    ("y", "x", 9, 5, -1),
-    ("x", "y", 14, 4, -1),
-    ("x", "y", 18, 5, 1),
-    ("y", "x", 23, 4, 1),
+    ((1,), "yzx", 0, 4, 1),
+    ((1,), "yzx", 4, 6, -1),
+    ((1,), "yzx", 10, 4, -1),
+    ((1,), "xzy", 14, 4, 1),
+    ((0,), "xzy", 0, 6, -1),
+    ((0,), "xzy", 6, 6, 1),
+    ((0,), "xzy", 12, 6, -1),
+    ((0, 1), "yzx", 18, 3, 1),
+    ((0, 1), "yzx", 21, 3, 1),
+    ((0, 1), "zxy", 24, 3, -1),
 )
 
 
-BYTES_PER_US = 65000.0
-SEND_US, HOP_US, STEP_US, CONVOLVE_US = 1.5, 0.3, 0.15, 0.45
+BYTES_PER_US = 54000.0
+SEND_US, HOP_US, STEP_US = 1.75, 0.3, 0.15
+CONVOLVE_US, TERMS_US, SHIFT_US = 0.45, 1.0, 1.5
 
 
 class Links:
@@ -78,13 +83,19 @@
         return handle
 
 
-def piece(ref, axes, at, lanes):
-    rows = pl.ds(0, 128)
-    if "z" in axes:
-        rows = pl.ds(pl.multiple_of(at["z"] * 16, 16), 16)
-    lead = [a for a in axes if a != "z"]
-    first = at[lead[0]] if lead else slice(None)
-    return ref.at[first, rows, lanes]
+def piece(ref, part, axes, at):
+    which, order, tap, taps, _ = part
+    split = [axis for axis in order[:2] if axis != "z"][0]
+    rows = pl.ds(pl.multiple_of(at["z"] * 16, 16), 16) if "z" in axes else slice(None)
+    lanes = pl.ds(tap * TAP_LANES, taps * TAP_LANES)
+    if split not in axes:
+        return ref.at[pl.ds(2 * which[0], 2 * len(which)), rows, lanes]
+    if len(which) == 2:
+        return ref.at[at[split], rows, lanes]
+    half = taps // 2
+    begin = (tap + at[split] % 2 * half) * TAP_LANES
+    lanes = pl.ds(pl.multiple_of(begin, TAP_LANES), half * TAP_LANES)
+    return ref.at[2 * which[0] + at[split] // 2, rows, lanes]
 
 
 ROUTES = {4: ((2, 1), (-1, -1)), 8: ((4, 1), (2, 1), (-3, -1), (-1, -1))}
@@ -145,22 +156,24 @@
 
 
 def reduce_part(links, part, source, result, buffers):
-    first, third, tap, taps, sense = part
-    lanes = pl.ds(tap * TAP_LANES, taps * TAP_LANES)
+    which, (first, second, third), tap, taps, sense = part
     stage_one, landing_one, sum_one, stage_two, landing_two, landing_three = buffers
+    at = links.at
 
     def own_first(index):
-        return source[index, :, lanes]
+        return piece(source, part, (first,), {first: index})[...]
 
     sum_one[...] = yield from scatter_axis(
         links, first, sense, own_first, stage_one, landing_one
     )
 
     def own_second(index):
-        return sum_one[pl.ds(pl.multiple_of(index * 16, 16), 16), :]
-
-    total = yield from scatter_axis(links, "z", -sense, own_second, stage_two, landing_two)
-    mine = landing_three.at[links.at[third]]
+        if second == "z":
+            return sum_one[pl.ds(pl.multiple_of(index * 16, 16), 16), :]
+        return sum_one[index]
+
+    total = yield from scatter_axis(links, second, -sense, own_second, stage_two, landing_two)
+    mine = landing_three.at[at[third]]
     mine[...] = total.astype(jnp.bfloat16)
     sent = [links.copy(mine, mine, third, shift) for shift in (1, -1, 2)]
     yield max(due for _, due in sent)
@@ -169,26 +182,28 @@
     total = landing_three[0].astype(jnp.float32)
     for index in range(1, EXTENT[third]):
         total = total + landing_three[index].astype(jnp.float32)
-    at = links.at
-    piece(result, (first, "z"), at, lanes)[...] = total.astype(jnp.bfloat16)
+    both = (first, second)
+    piece(result, part, both, at)[...] = total.astype(jnp.bfloat16)
     yield from gather_axis(
-        links, "z", sense, lambda index: piece(result, (first, "z"), {**at, "z": index}, lanes)
+        links, second, sense, lambda index: piece(result, part, both, {**at, second: index})
     )
     yield from gather_axis(
-        links, first, -sense, lambda index: piece(result, (first,), {first: index}, lanes)
+        links, first, -sense, lambda index: piece(result, part, (first,), {first: index})
     )
 
 
 def part_scratch(part):
-    first, third, tap, taps, sense = part
-    one, two = (128, taps * TAP_LANES), (16, taps * TAP_LANES)
+    which, (first, second, third), tap, taps, sense = part
+    lanes = taps * TAP_LANES * len(which) // 2
+    two = (16, lanes)
+    one = (4,) + two if first == "z" else (128, lanes)
     slots = {axis: EXTENT[axis] - 1 for axis in EXTENT}
     return [
         pltpu.VMEM((slots[first],) + one, jnp.bfloat16),
         pltpu.VMEM((slots[first],) + one, jnp.bfloat16),
         pltpu.VMEM(one, jnp.float32),
-        pltpu.VMEM((slots["z"],) + two, jnp.bfloat16),
-        pltpu.VMEM((slots["z"],) + two, jnp.bfloat16),
+        pltpu.VMEM((slots[second],) + two, jnp.bfloat16),
+        pltpu.VMEM((slots[second],) + two, jnp.bfloat16),
         pltpu.VMEM((EXTENT[third],) + two, jnp.bfloat16),
     ]
 
@@ -359,6 +374,7 @@
     turned,
     mine,
     terms,
+    held,
     *buffers,
 ):
     links = Links(send_sems, recv_sems)
@@ -421,17 +437,45 @@
     swap = links.send(back.at[1 - core], back_other, links.beside(0, 1 - core))
     own_cot = cot_level[1, cells].reshape(CELLS_CHIP, HALF).astype(jnp.float32)
     turned[1] = own_cot.T.astype(jnp.bfloat16)
-    swap.wait_recv()
-    values = pre[...]
-    sigma = jax.nn.sigmoid(values)
-    slope = (back[core] + back_other[...]) * (sigma * (1.0 + values * (1.0 - sigma)))
-    turned[0] = slope.T.astype(jnp.bfloat16)
-    for along_az in range(3):
-        weight_terms(turned.at[0], in_level, in_padded, terms, 0, along_az)
     for handle in field_hid:
         handle.wait_recv()
     shifted_copies(hid_level, hid_padded)
-    waiting, used = [], 0
+    parts, used = [], 0
+    for part in PARTS:
+        count = len(part_scratch(part))
+        parts.append((part, buffers[used : used + count]))
+        used += count
+    stored = []
+
+    def one_part(part, scratch):
+        yield from reduce_part(links, part, terms, held, scratch)
+        done = [piece(ref, part, (), {}) for ref in (held, result)]
+        stored.append(pltpu.make_async_copy(*done, local_sems.at[4 + len(stored)]))
+        stored[-1].start()
+
+    def gradients():
+        ready = set()
+        for which in (1, 0):
+            if which == 0:
+                swap.wait_recv()
+                values = pre[...]
+                sigma = jax.nn.sigmoid(values)
+                slope = (back[core] + back_other[...]) * (sigma * (1.0 + values * (1.0 - sigma)))
+                turned[0] = slope.T.astype(jnp.bfloat16)
+            level, padded = (in_level, in_padded) if which == 0 else (hid_level, hid_padded)
+            for along_az in range(3):
+                weight_terms(turned.at[which], level, padded, terms, which, along_az)
+                links.now += TERMS_US
+                ready |= {(which, 9 * along_az + tap) for tap in range(9)}
+                for one in list(parts):
+                    grads, _, tap, taps, _ = one[0]
+                    if {(g, t) for g in grads for t in range(tap, tap + taps)} <= ready:
+                        parts.remove(one)
+                        advance(one_part(*one))
+                yield 0.0
+        advance(flow_part(links, in_level, hid_level, hid_padded, second_rows, second, mine, flow))
+
+    waiting = []
 
     def advance(one):
         links.now += STEP_US
@@ -440,25 +484,20 @@
         except StopIteration:
             pass
 
-    for part in PARTS:
-        if part[2] % 9 == 0:
-            weight_terms(turned.at[1], hid_level, hid_padded, terms, 1, part[2] // 9)
-            links.now += 1.0
-        count = len(part_scratch(part))
-        advance(reduce_part(links, part, terms, result, buffers[used : used + count]))
-        used += count
-    advance(flow_part(links, in_level, hid_level, hid_padded, second_rows, second, mine, flow))
+    advance(gradients())
     while waiting:
-        due = [links.now + CONVOLVE_US if at is None else at for at, _ in waiting]
+        due = [links.now + CONVOLVE_US if at is None else at or links.now for at, _ in waiting]
         soonest = min(range(len(due)), key=due.__getitem__)
         at, one = waiting.pop(soonest)
         links.now = max(links.now, at or 0.0)
         advance(one)
+    for copy in stored:
+        copy.wait()
     for handle in links.started:
         handle.wait_send()
 
 
-COPIES = 192
+COPIES = 256
 
 
 def whole_layer(features, cotangent, w_first, w_second):
@@ -467,7 +506,7 @@
     scratch = [
         pltpu.SemaphoreType.DMA((COPIES,)),
         pltpu.SemaphoreType.DMA((COPIES,)),
-        pltpu.SemaphoreType.DMA((4,)),
+        pltpu.SemaphoreType.DMA((4 + len(PARTS),)),
         pltpu.VMEM((HALF, TAPS * CH), jnp.bfloat16),
         pltpu.VMEM((HALF, TAPS * CH), jnp.bfloat16),
         pltpu.VMEM(field + (CH,), jnp.bfloat16),
@@ -483,6 +522,7 @@
         pltpu.VMEM((2, HALF, CELLS_CHIP), jnp.bfloat16),
         pltpu.VMEM((AZ_DEV, ROWS, HALF), jnp.bfloat16),
         pltpu.VMEM((4, HALF, TAPS * HALF), jnp.float32),
+        pltpu.VMEM((4, HALF, TAPS * HALF), jnp.bfloat16),
     ]
     for part in PARTS:
         scratch += part_scratch(part)
@@ -493,7 +533,7 @@
             jax.ShapeDtypeStruct((4, HALF, TAPS * HALF), jnp.bfloat16),
         ),
         in_specs=[pl.BlockSpec(memory_space=pl.ANY)] * 4,
-        out_specs=(pl.BlockSpec(memory_space=pltpu.VMEM), pl.BlockSpec(memory_space=pltpu.VMEM)),
+        out_specs=(pl.BlockSpec(memory_space=pltpu.VMEM), pl.BlockSpec(memory_space=pl.ANY)),
         scratch_shapes=scratch,
         compiler_params=pltpu.CompilerParams(
             collective_id=0, has_side_effects=True, vmem_limit_bytes=56 * 2**20
@@ -531,7 +571,7 @@
             pl.BlockSpec((HALF, third), lambda g, p: (0, jnp.where(g == 0, p, 2))),
             pl.BlockSpec((HALF, third), lambda g, p: (0, jnp.where(g == 0, 0, p))),
         ),
-        compiler_params=pltpu.CompilerParams(vmem_limit_bytes=24 * 2**20),
+        compiler_params=pltpu.CompilerParams(vmem_limit_bytes=60 * 2**20),
         name="widen",
     )(summed)
 

time: 97.5 us -> 92.8 us (0.952); the launches traced: 95.7 us -> 92.1 us
  local copies, waits for them, and re-layouts: 2.65 us -> 0.66 us
  Pallas kernels: 92.4 us -> 90.8 us
    pallas_call x1, Pallas kernels: 88.2 us -> 84.4 us  [whole_layer(): pl.pallas_call(whole_kernel, out_shape=(jax.ShapeDtypeStruct((AZ_DEV, OWN...]
    pallas_call x1, Pallas kernels: 4.25 us -> 6.44 us  [widen(): pl.pallas_call(functools.partial(widen_kernel, factor), grid=(2, 3), out_...]
    unnamed x5 -> x3, local copies, waits for them, and re-layouts: 2.65 us -> 0.66 us
where the time goes in v4:
time: 92.8 us; the launch traced here: 92.1 us
  Pallas kernels  90.8 us (98%)
    pallas_call x1, Pallas kernels, whole_layer(): pl.pallas_call(whole_kernel, out_shape=(jax.ShapeDtypeStruct((AZ_DEV, OWN...  84.4 us
    pallas_call x1, Pallas kernels, widen(): pl.pallas_call(functools.partial(widen_kernel, factor), grid=(2, 3), out_...  6.44 us

profile of v4, /device:TPU:8, one launch (start us, length us, event | category | flops | bytes accessed | tf_op | source)
XLA Modules:
  0.0 92.1 jit_solution(7195069965580194492)
XLA Ops:
  0.6 84.4 %both_layers.1 = (bf16[4,64,256]{2,1,0:T(8,128)(2,1)}, bf16[4,128,3456]{2,1,0:T(8,128)(2,1)}) custom-call(bf16[4,64,256]{2,1,0:T(8,128)(2,1)} %bitcast.4, bf16[4,64,256]{2,1,0:T(8,128)(2,1)} %bitcast.5, bf16[128,6912]{1,0:T(8,128)(2,1)} %w_first.1, bf16[128,6912]{1,0:T(8,128)(2,1)} %w_second.1), custom_call_target="tpu_custom_call" | custom-call | tf_op jit(solution)/shard_map/both_layers/pallas_call | solution.py:529
  85.0 0.0 copy-start
  85.0 6.4 %widen.1 = (f32[128,6912]{1,0:T(8,128)}, f32[128,6912]{1,0:T(8,128)}) custom-call(bf16[4,128,3456]{2,1,0:T(8,128)(2,1)} %get-tuple-element.8.summed), custom_call_target="tpu_custom_call" | custom-call | tf_op jit(solution)/shard_map/widen/pallas_call | solution.py:565
  91.5 0.0 copy-done
  91.5 0.7 copy.8
Async XLA Ops:
  85.0 6.5 %copy-start = (bf16[4,64,256]{2,1,0:T(8,128)(2,1)S(1)}, bf16[4,64,256]{2,1,0:T(8,128)(2,1)}, u32[]{:S(2)}) copy-start(bf16[4,64,256]{2,1,0:T(8,128)(2,1)} %get-tuple-element.7) | copy-start | bytes 393220

commit v5 on v4

--- a/solution.py
+++ b/solution.py
@@ -22,16 +22,16 @@
 EXTENT = {"x": NX, "y": NY, "z": NZ}
 TAP_LANES = 128
 PARTS = (
-    ((1,), "yzx", 0, 4, 1),
-    ((1,), "yzx", 4, 6, -1),
-    ((1,), "yzx", 10, 4, -1),
-    ((1,), "xzy", 14, 4, 1),
-    ((0,), "xzy", 0, 6, -1),
-    ((0,), "xzy", 6, 6, 1),
-    ((0,), "xzy", 12, 6, -1),
+    ((1,), "yzx", 0, 2, 1),
+    ((1,), "xzy", 2, 4, 1),
+    ((1,), "xzy", 6, 6, -1),
+    ((1,), "yzx", 12, 6, 1),
+    ((0,), "xzy", 0, 6, 1),
+    ((0,), "xzy", 6, 6, -1),
+    ((0,), "yzx", 12, 6, -1),
     ((0, 1), "yzx", 18, 3, 1),
     ((0, 1), "yzx", 21, 3, 1),
-    ((0, 1), "zxy", 24, 3, -1),
+    ((0, 1), "xzy", 24, 3, 1),
 )
 
 
@@ -532,7 +532,7 @@
             jax.ShapeDtypeStruct((AZ_DEV, OWN_ROWS, CH), jnp.bfloat16),
             jax.ShapeDtypeStruct((4, HALF, TAPS * HALF), jnp.bfloat16),
         ),
-        in_specs=[pl.BlockSpec(memory_space=pl.ANY)] * 4,
+        in_specs=[pl.BlockSpec(memory_space=pltpu.HBM)] * 4,
         out_specs=(pl.BlockSpec(memory_space=pltpu.VMEM), pl.BlockSpec(memory_space=pl.ANY)),
         scratch_shapes=scratch,
         compiler_params=pltpu.CompilerParams(
@@ -542,36 +542,47 @@
     )(features, cotangent, w_first, w_second)
 
 
-def widen_kernel(factor, summed, grad_first, grad_second):
-    def put(target):
-        for tap in range(9):
+def widen_kernel(factor, summed, grad_first, grad_second, taken, wide, in_sems, out_sems):
+    pieces = [(which, third) for which in range(2) for third in range(3)]
+    loads, stores = [], []
+    for number, (which, third) in enumerate(pieces):
+        view = (pl.ds(2 * which, 2), slice(None), pl.ds(third * 9 * HALF, 9 * HALF))
+        loads.append(
+            pltpu.make_async_copy(summed.at[view], taken.at[view], in_sems.at[number])
+        )
+        loads[-1].start()
+    for number, (which, third) in enumerate(pieces):
+        loads[number].wait()
+        for tap in range(9 * third, 9 * third + 9):
             for side in range(2):
-                target[:, (2 * tap + side) * HALF : (2 * tap + side + 1) * HALF] = (
-                    summed[side, :, tap * HALF : (tap + 1) * HALF].astype(jnp.float32) * factor
+                wide[which, :, (2 * tap + side) * HALF : (2 * tap + side + 1) * HALF] = (
+                    taken[2 * which + side, :, tap * HALF : (tap + 1) * HALF].astype(jnp.float32)
+                    * factor
                 )
-
-    @pl.when(pl.program_id(0) == 0)
-    def _():
-        put(grad_first)
-
-    @pl.when(pl.program_id(0) == 1)
-    def _():
-        put(grad_second)
+        view = (slice(None), pl.ds(third * 9 * CH, 9 * CH))
+        target = grad_second if which else grad_first
+        stores.append(
+            pltpu.make_async_copy(wide.at[which].at[view], target.at[view], out_sems.at[number])
+        )
+        stores[-1].start()
+    for store in stores:
+        store.wait()
 
 
 def widen(summed, factor):
-    third = TAPS * CH // 3
     shape = jax.ShapeDtypeStruct((HALF, TAPS * CH), jnp.float32)
     return pl.pallas_call(
         functools.partial(widen_kernel, factor),
-        grid=(2, 3),
         out_shape=(shape, shape),
-        in_specs=[pl.BlockSpec((2, HALF, third // 2), lambda g, p: (g, 0, p))],
-        out_specs=(
-            pl.BlockSpec((HALF, third), lambda g, p: (0, jnp.where(g == 0, p, 2))),
-            pl.BlockSpec((HALF, third), lambda g, p: (0, jnp.where(g == 0, 0, p))),
-        ),
-        compiler_params=pltpu.CompilerParams(vmem_limit_bytes=60 * 2**20),
+        in_specs=[pl.BlockSpec(memory_space=pl.ANY)],
+        out_specs=(pl.BlockSpec(memory_space=pl.ANY), pl.BlockSpec(memory_space=pl.ANY)),
+        scratch_shapes=[
+            pltpu.VMEM((4, HALF, TAPS * HALF), jnp.bfloat16),
+            pltpu.VMEM((2, HALF, TAPS * CH), jnp.float32),
+            pltpu.SemaphoreType.DMA((6,)),
+            pltpu.SemaphoreType.DMA((6,)),
+        ],
+        compiler_params=pltpu.CompilerParams(vmem_limit_bytes=58 * 2**20),
         name="widen",
     )(summed)
 

time: 92.8 us -> 90.5 us (0.975)
  Pallas kernels: 90.8 us -> 88.7 us
    pallas_call x1, Pallas kernels: 6.44 us -> 4.2 us  [widen(): pl.pallas_call(functools.partial(widen_kernel, factor), out_shape=(shape,...]
where the time goes in v5:
time: 90.5 us; the launch traced here: 90 us
  Pallas kernels  88.7 us (98%)
    pallas_call x1, Pallas kernels, whole_layer(): pl.pallas_call(whole_kernel, out_shape=(jax.ShapeDtypeStruct((AZ_DEV, OWN...  84.5 us
    pallas_call x1, Pallas kernels, widen(): pl.pallas_call(functools.partial(widen_kernel, factor), out_shape=(shape,...  4.2 us

profile of v5, /device:TPU:8, one launch (start us, length us, event | category | flops | bytes accessed | tf_op | source)
XLA Modules:
  0.0 90.0 jit_solution(16246383581522369318)
XLA Ops:
  0.6 84.5 %both_layers.1 = (bf16[4,64,256]{2,1,0:T(8,128)(2,1)}, bf16[4,128,3456]{2,1,0:T(8,128)(2,1)}) custom-call(bf16[4,64,256]{2,1,0:T(8,128)(2,1)} %bitcast.4, bf16[4,64,256]{2,1,0:T(8,128)(2,1)} %bitcast.5, bf16[128,6912]{1,0:T(8,128)(2,1)} %w_first.1, bf16[128,6912]{1,0:T(8,128)(2,1)} %w_second.1), custom_call_target="tpu_custom_call" | custom-call | tf_op jit(solution)/shard_map/both_layers/pallas_call | solution.py:529
  85.1 0.0 copy-start
  85.1 4.2 %widen.1 = (f32[128,6912]{1,0:T(8,128)}, f32[128,6912]{1,0:T(8,128)}) custom-call(bf16[4,128,3456]{2,1,0:T(8,128)(2,1)} %get-tuple-element.8.summed), custom_call_target="tpu_custom_call" | custom-call | tf_op jit(solution)/shard_map/widen/pallas_call | solution.py:574
  89.3 0.0 copy-done
  89.3 0.7 copy.8
Async XLA Ops:
  85.1 4.2 %copy-start = (bf16[4,64,256]{2,1,0:T(8,128)(2,1)S(1)}, bf16[4,64,256]{2,1,0:T(8,128)(2,1)}, u32[]{:S(2)}) copy-start(bf16[4,64,256]{2,1,0:T(8,128)(2,1)} %get-tuple-element.7) | copy-start | bytes 393220

commit v6 on v5

--- a/solution.py
+++ b/solution.py
@@ -542,7 +542,19 @@
     )(features, cotangent, w_first, w_second)
 
 
-def widen_kernel(factor, summed, grad_first, grad_second, taken, wide, in_sems, out_sems):
+def widen_kernel(
+    factor,
+    summed,
+    flow,
+    grad_first,
+    grad_second,
+    flow_out,
+    taken,
+    wide,
+    held,
+    in_sems,
+    out_sems,
+):
     pieces = [(which, third) for which in range(2) for third in range(3)]
     loads, stores = [], []
     for number, (which, third) in enumerate(pieces):
@@ -551,6 +563,8 @@
             pltpu.make_async_copy(summed.at[view], taken.at[view], in_sems.at[number])
         )
         loads[-1].start()
+    flow_in = pltpu.make_async_copy(flow, held, in_sems.at[len(pieces)])
+    flow_in.start()
     for number, (which, third) in enumerate(pieces):
         loads[number].wait()
         for tap in range(9 * third, 9 * third + 9):
@@ -565,26 +579,30 @@
             pltpu.make_async_copy(wide.at[which].at[view], target.at[view], out_sems.at[number])
         )
         stores[-1].start()
+    flow_in.wait()
+    stores.append(pltpu.make_async_copy(held, flow_out, out_sems.at[len(pieces)]))
+    stores[-1].start()
     for store in stores:
         store.wait()
 
 
-def widen(summed, factor):
+def widen(summed, flow, factor):
     shape = jax.ShapeDtypeStruct((HALF, TAPS * CH), jnp.float32)
     return pl.pallas_call(
         functools.partial(widen_kernel, factor),
-        out_shape=(shape, shape),
-        in_specs=[pl.BlockSpec(memory_space=pl.ANY)],
-        out_specs=(pl.BlockSpec(memory_space=pl.ANY), pl.BlockSpec(memory_space=pl.ANY)),
+        out_shape=(shape, shape, jax.ShapeDtypeStruct(flow.shape, flow.dtype)),
+        in_specs=[pl.BlockSpec(memory_space=pl.ANY)] * 2,
+        out_specs=(pl.BlockSpec(memory_space=pl.ANY),) * 3,
         scratch_shapes=[
             pltpu.VMEM((4, HALF, TAPS * HALF), jnp.bfloat16),
             pltpu.VMEM((2, HALF, TAPS * CH), jnp.float32),
-            pltpu.SemaphoreType.DMA((6,)),
-            pltpu.SemaphoreType.DMA((6,)),
+            pltpu.VMEM(flow.shape, flow.dtype),
+            pltpu.SemaphoreType.DMA((7,)),
+            pltpu.SemaphoreType.DMA((7,)),
         ],
         compiler_params=pltpu.CompilerParams(vmem_limit_bytes=58 * 2**20),
         name="widen",
-    )(summed)
+    )(summed, flow)
 
 
 def local(features, cotangent, w_first, w_second):
@@ -592,7 +610,7 @@
     flow, summed = whole_layer(
         features.transpose(1, 2, 0), cotangent.transpose(1, 2, 0), w_first, w_second
     )
-    grad_first, grad_second = widen(summed, factor)
+    grad_first, grad_second, flow = widen(summed, flow, factor)
     return (flow.transpose(2, 0, 1), grad_first, grad_second)
 
 

time: 90.5 us -> 89.8 us (level)
  no operation moved by 1% of the time
where the time goes in v6:
time: 89.8 us; the launch traced here: 89.3 us
  Pallas kernels  88.7 us (99%)
    pallas_call x1, Pallas kernels, whole_layer(): pl.pallas_call(whole_kernel, out_shape=(jax.ShapeDtypeStruct((AZ_DEV, OWN...  84.5 us
    pallas_call x1, Pallas kernels, widen(): pl.pallas_call(functools.partial(widen_kernel, factor), out_shape=(shape,...  4.19 us

profile of v6, /device:TPU:8, one launch (start us, length us, event | category | flops | bytes accessed | tf_op | source)
XLA Modules:
  0.0 89.3 jit_solution(3076340486120807942)
XLA Ops:
  0.6 84.5 %both_layers.1 = (bf16[4,64,256]{2,1,0:T(8,128)(2,1)}, bf16[4,128,3456]{2,1,0:T(8,128)(2,1)}) custom-call(bf16[4,64,256]{2,1,0:T(8,128)(2,1)} %bitcast.3, bf16[4,64,256]{2,1,0:T(8,128)(2,1)} %bitcast.4, bf16[128,6912]{1,0:T(8,128)(2,1)} %w_first.1, bf16[128,6912]{1,0:T(8,128)(2,1)} %w_second.1), custom_call_target="tpu_custom_call" | custom-call | tf_op jit(solution)/shard_map/both_layers/pallas_call | solution.py:529
  85.1 4.2 %widen.1 = (f32[128,6912]{1,0:T(8,128)}, f32[128,6912]{1,0:T(8,128)}, bf16[4,64,256]{2,1,0:T(8,128)(2,1)}) custom-call(bf16[4,128,3456]{2,1,0:T(8,128)(2,1)} %get-tuple-element.8.summed, bf16[4,64,256]{2,1,0:T(8,128)(2,1)} %get-tuple-element.9.flow), custom_call_target="tpu_custom_call" | custom-call | tf_op jit(solution)/shard_map/widen/pallas_call | solution.py:591

commit v7 on v6

--- a/solution.py
+++ b/solution.py
@@ -101,23 +101,31 @@
 ROUTES = {4: ((2, 1), (-1, -1)), 8: ((4, 1), (2, 1), (-3, -1), (-1, -1))}
 
 
-def relays(axis):
-    return [(owner - stop, stop) for owner, stop in ROUTES[EXTENT[axis]] if owner != stop]
-
-
-def arrivals(axis):
-    routes = ROUTES[EXTENT[axis]]
-    return [onward for onward, _ in relays(axis)] + [o for o, stop in routes if o == stop]
-
-
-def scatter_axis(links, axis, sense, own, stage, landing):
+STRAIGHT = ((2, 2), (1, 1), (-1, -1))
+HASTY = (6,)
+
+
+def routes_of(axis, hasty):
+    return STRAIGHT if hasty else ROUTES[EXTENT[axis]]
+
+
+def relays(axis, hasty):
+    return [(owner - stop, stop) for owner, stop in routes_of(axis, hasty) if owner != stop]
+
+
+def arrivals(axis, hasty):
+    routes = routes_of(axis, hasty)
+    return [onward for onward, _ in relays(axis, hasty)] + [o for o, stop in routes if o == stop]
+
+
+def scatter_axis(links, axis, sense, own, stage, landing, hasty=False):
     first = []
-    for slot, (owner, stop) in enumerate(ROUTES[EXTENT[axis]]):
+    for slot, (owner, stop) in enumerate(routes_of(axis, hasty)):
         stage[slot] = own(links.index(axis, sense * owner)).astype(jnp.bfloat16)
         first.append(links.copy(stage.at[slot], landing.at[slot], axis, sense * stop))
     last = []
     slot = len(first)
-    for number, (owner, stop) in enumerate(ROUTES[EXTENT[axis]]):
+    for number, (owner, stop) in enumerate(routes_of(axis, hasty)):
         handle, due = first[number]
         if owner == stop:
             last.append((number, handle, due))
@@ -137,13 +145,13 @@
     return total
 
 
-def gather_axis(links, axis, sense, view):
+def gather_axis(links, axis, sense, view, hasty=False):
     chunk = view(links.at[axis])
     first = [
-        (onward,) + links.copy(chunk, chunk, axis, sense * onward) for onward in arrivals(axis)
+        (onward,) + links.copy(chunk, chunk, axis, sense * onward) for onward in arrivals(axis, hasty)
     ]
     last = []
-    for number, (onward, stop) in enumerate(relays(axis)):
+    for number, (onward, stop) in enumerate(relays(axis, hasty)):
         _, handle, due = first[number]
         yield due
         handle.wait_recv()
@@ -159,12 +167,13 @@
     which, (first, second, third), tap, taps, sense = part
     stage_one, landing_one, sum_one, stage_two, landing_two, landing_three = buffers
     at = links.at
+    hasty = PARTS.index(part) in HASTY
 
     def own_first(index):
         return piece(source, part, (first,), {first: index})[...]
 
     sum_one[...] = yield from scatter_axis(
-        links, first, sense, own_first, stage_one, landing_one
+        links, first, sense, own_first, stage_one, landing_one, hasty
     )
 
     def own_second(index):
@@ -188,7 +197,7 @@
         links, second, sense, lambda index: piece(result, part, both, {**at, second: index})
     )
     yield from gather_axis(
-        links, first, -sense, lambda index: piece(result, part, (first,), {first: index})
+        links, first, -sense, lambda index: piece(result, part, (first,), {first: index}), hasty
     )
 
 

time: 89.8 us -> 91.4 us (1.018)
  Pallas kernels: 88.7 us -> 90.7 us
    pallas_call x1, Pallas kernels: 84.5 us -> 86.5 us  [whole_layer(): pl.pallas_call(whole_kernel, out_shape=(jax.ShapeDtypeStruct((AZ_DEV, OWN...]
where the time goes in v7:
time: 91.4 us; the launch traced here: 91.3 us
  Pallas kernels  90.7 us (99%)
    pallas_call x1, Pallas kernels, whole_layer(): pl.pallas_call(whole_kernel, out_shape=(jax.ShapeDtypeStruct((AZ_DEV, OWN...  86.5 us
    pallas_call x1, Pallas kernels, widen(): pl.pallas_call(functools.partial(widen_kernel, factor), out_shape=(shape,...  4.19 us

profile of v7, /device:TPU:8, one launch (start us, length us, event | category | flops | bytes accessed | tf_op | source)
XLA Modules:
  0.0 91.3 jit_solution(16285557347148903679)
XLA Ops:
  0.6 86.5 %both_layers.1 = (bf16[4,64,256]{2,1,0:T(8,128)(2,1)}, bf16[4,128,3456]{2,1,0:T(8,128)(2,1)}) custom-call(bf16[4,64,256]{2,1,0:T(8,128)(2,1)} %bitcast.3, bf16[4,64,256]{2,1,0:T(8,128)(2,1)} %bitcast.4, bf16[128,6912]{1,0:T(8,128)(2,1)} %w_first.1, bf16[128,6912]{1,0:T(8,128)(2,1)} %w_second.1), custom_call_target="tpu_custom_call" | custom-call | tf_op jit(solution)/shard_map/both_layers/pallas_call | solution.py:538
  87.2 4.2 %widen.1 = (f32[128,6912]{1,0:T(8,128)}, f32[128,6912]{1,0:T(8,128)}, bf16[4,64,256]{2,1,0:T(8,128)(2,1)}) custom-call(bf16[4,128,3456]{2,1,0:T(8,128)(2,1)} %get-tuple-element.8.summed, bf16[4,64,256]{2,1,0:T(8,128)(2,1)} %get-tuple-element.9.flow), custom_call_target="tpu_custom_call" | custom-call | tf_op jit(solution)/shard_map/widen/pallas_call | solution.py:600
